TPU v7x, 128 devices: a whole 4x4x4 slice. The times are simulated.
128 devices in a mesh: group: 4 (over y_lo, core), fsdp: 32 (over y_hi, x, z).
Axes of the slice: x: 4, y: 4 (y_hi: 2, y_lo: 2; y = y_hi * 2 + y_lo), z: 4, core: 2. Of those that a mesh axis runs over, the one named last changes fastest.
Arguments:
- grads: float32 [128, 4, 1048576], P(('group', 'fsdp')), may hold values from -24 to 24
- params: float32 [4, 1048576], P('group', 'fsdp'), may hold values from -6 to 6
- moment_one: float32 [4, 1048576], P('group', 'fsdp'), may hold values from -18 to 18
- moment_two: float32 [4, 1048576], P('group', 'fsdp'), may hold values from 1 to 100
- coding: float32 [4, 2], replicated, as said below
- holders: int32 [32, 2], P('fsdp'), may hold values from 0 to 3, as said below
Outputs:
- new_params: float32 [4, 1048576], P('group', 'fsdp')
- new_moment_one: float32 [4, 1048576], P('group', 'fsdp')
- new_moment_two: float32 [4, 1048576], P('group', 'fsdp')
- parity_held: float32 [4, 1048576], P('group', 'fsdp')
Inputs may be any that keep to these rules, and one draw needn't show every extreme that they name: `holders`: the two groups of a slot differ. coding[g, k] = 1 / (x_g + y_k) with distinct positive x_g and y_k.
All inputs are finite; a program needn't handle non-finite values.
Results may differ from a plain program's by a relative error of at most 0.000071.
Values sent between devices are 32-bit elements; how exact they have to be, the bound alone decides.
A program may use at most 128 MiB of HBM per device.

v0:
```python
import jax
import jax.numpy as jnp
from jax import lax
from jax.sharding import PartitionSpec as P


def shards(grads, params, moment_one, moment_two, coding, holders):
    groups = lax.axis_size("group")
    slot_count = lax.axis_size("fsdp")
    shard_length = params.shape[1]
    partial_row = grads[0]
    gradient = lax.psum_scatter(
        partial_row.reshape(1, groups * slot_count * shard_length),
        ("group", "fsdp"),
        scatter_dimension=1,
        tiled=True,
    )
    first_moment = 0.9 * moment_one + 0.1 * gradient
    second_moment = 0.95 * moment_two + 0.05 * gradient * gradient
    first_fix = 1.0 - 0.9**10
    second_fix = 1.0 - 0.95**10
    update = (
        first_moment / first_fix / (jnp.sqrt(second_moment / second_fix) + 1e-08) + 0.1 * params
    )
    new_params = params - 0.05 * update
    my_group = lax.axis_index("group")
    group_numbers = jnp.arange(groups, dtype=jnp.int32)
    group_mask = (group_numbers == my_group).astype(jnp.float32)
    my_coding = jnp.sum(coding * group_mask[:, None], axis=0)
    my_holders = holders[0]
    weighted = my_coding[:, None] * new_params
    parity_totals = lax.psum(weighted, "group")
    selection = (my_holders == my_group).astype(jnp.float32)
    parity_held = jnp.sum(selection[:, None] * parity_totals, axis=0, keepdims=True)
    return (new_params, first_moment, second_moment, parity_held)


def solution(mesh):
    return jax.shard_map(
        shards,
        mesh=mesh,
        in_specs=(
            P(("group", "fsdp"), None, None),
            P("group", "fsdp"),
            P("group", "fsdp"),
            P("group", "fsdp"),
            P(),
            P("fsdp", None),
        ),
        out_specs=(P("group", "fsdp"), P("group", "fsdp"), P("group", "fsdp"), P("group", "fsdp")),
        check_vma=False,
    )
```

profile of v0, /device:TPU:1, one launch (start us, length us, event | category | flops | bytes accessed | tf_op | source)
XLA Modules:
  0.0 294.3 jit_solution(2448128666664479310)
XLA Ops:
  7.2 0.0 all-reduce.6.cloned.1.call-start
  7.2 19.8 %copy.12 = f32[1,1,4,1048576]{3,1,2,0:T(1,128)} copy(f32[1,1,4,1048576]{3,2,1,0:T(4,128)} %bitcast.9) | data formatting | bytes 33554432
  27.1 0.0 copy-start.4
  27.1 0.0 copy-start.1
  27.1 0.0 copy-start.2
  27.1 0.0 copy-start.3
  27.1 0.0 copy-start.5
  27.1 0.0 all-reduce.6.cloned.1.call-update
  27.1 0.0 all-reduce.4.cloned.1.call-start
  27.2 0.5 copy-done.4
  27.7 0.1 multiply_reduce_fusion.1
  27.9 219.4 %all-reduce.6.cloned.1.call-done = f32[1,4194304]{1,0:T(1,128)} async-done(((f32[1,4194304]{1,0:T(1,128)}), f32[1,4194304]{1,0:T(1,128)}) %all-reduce.6.cloned.1.call-update) | async-done | bytes 16777232
  247.2 0.0 copy-done.1
  247.2 0.0 copy-done.2
  247.2 0.0 copy-done.3
  247.2 2.4 multiply_subtract_fusion
  249.6 0.0 copy-start
  249.6 0.8 broadcast_multiply_fusion
  250.5 0.0 all-reduce.4.cloned.1.call-update
  250.5 0.0 copy-done.5
  250.5 34.9 %all-reduce.4.cloned.1.call-done = f32[2,32768]{1,0:T(2,128)} async-done(((f32[2,32768]{1,0:T(2,128)}), f32[2,32768]{1,0:T(2,128)}) %all-reduce.4.cloned.1.call-update) | async-done | bytes 262160 | tf_op jit(solution)/shard_map/psum | solution.py:32
  285.5 2.0 multiply_reduce_fusion
  287.5 0.0 copy-done
  (2 shorter events, 0.0 us)
Async XLA Ops:
  7.2 240.1 %all-reduce.6.cloned.1.call-start = ((), (), s32[]{:S(2)}) async-start(), calls=%async_computation.1 | async-start | bytes 33554432
  27.1 0.7 copy-start.4
  27.1 220.2 %copy-start.1 = (f32[1,32768]{1,0:T(1,128)S(1)}, f32[1,32768]{1,0:T(1,128)}, u32[]{:S(2)}) copy-start(f32[1,32768]{1,0:T(1,128)} %param.7) | copy-start | bytes 393220
  27.1 220.2 %copy-start.2 = (f32[1,32768]{1,0:T(1,128)S(1)}, f32[1,32768]{1,0:T(1,128)}, u32[]{:S(2)}) copy-start(f32[1,32768]{1,0:T(1,128)} %param.8) | copy-start | bytes 393220
  27.1 220.2 %copy-start.3 = (f32[1,32768]{1,0:T(1,128)S(1)}, f32[1,32768]{1,0:T(1,128)}, u32[]{:S(2)}) copy-start(f32[1,32768]{1,0:T(1,128)} %param.9) | copy-start | bytes 393220
  27.1 223.4 %copy-start.5 = (s32[1,2]{1,0:T(1,128)S(1)}, s32[1,2]{1,0:T(1,128)}, u32[]{:S(2)}) copy-start(s32[1,2]{1,0:T(1,128)} %param.11) | copy-start | bytes 28
  27.1 258.4 %all-reduce.4.cloned.1.call-start = ((), (), s32[]{:S(2)}) async-start(), calls=%async_computation | async-start | bytes 524288 | tf_op jit(solution)/shard_map/psum | solution.py:32
  249.6 37.8 %copy-start = (f32[1,32768]{1,0:T(1,128)}, f32[1,32768]{1,0:T(1,128)S(1)}, u32[]{:S(2)}) copy-start(f32[1,32768]{1,0:T(1,128)S(1)} %get-tuple-element.4) | copy-start | bytes 393220
Sparse Core Ops, SparseCore 0:
  27.2 219.9 all-reduce.5
  250.6 34.7 all-reduce.3
where the time goes:
time: 294 us
  waiting for transfers between devices  254 us (86%)
  local copies, waits for them, and re-layouts  20.4 us (7%)
  between operations  14.1 us (5%)
  other arithmetic  5.39 us (2%)
    unnamed x3, waiting for transfers between devices  219 us
    psum x1, waiting for transfers between devices, shards(): parity_totals = lax.psum(weighted, 'group')  34.9 us
    unnamed x13, local copies, waits for them, and re-layouts  20.4 us
  transfers between devices with their start and end apart: 2, of which 2 were waited for; matrix products, arithmetic and copies ran while one was open for 0% of the time, Pallas kernels for 0%

commit v1 on v0

v1 whole, which is shorter than its diff:
```python
import functools
import jax
import jax.numpy as jnp
from jax import lax
from jax.experimental import pallas as pl
from jax.experimental.pallas import tpu as pltpu
from jax.sharding import PartitionSpec as P

MESH = pl.DeviceIdType.MESH
LANES = 128
STEP = (2, 3, 1, 0)
FAR, BEFORE, AFTER, OWN = range(4)
PARTS = (((0, 1, 2), 0, 88), ((1, 2, 0), 88, 80), ((2, 0, 1), 168, 88))
ROWS = 256
ONE = {"far": (0, 1), "near": (1, 2), "own": (3, 1)}
UNITS = tuple(
    (ONE[a], ONE[b])
    for a, b in (
        ("far", "far"),
        ("far", "near"),
        ("near", "far"),
        ("near", "near"),
        ("far", "own"),
        ("own", "far"),
        ("own", "near"),
        ("near", "own"),
        ("own", "own"),
    )
)
UNITS2 = ((ONE["far"],), (ONE["near"],), (ONE["own"],))
UNITS3 = ((),)
STAGES = (UNITS, UNITS2, UNITS3)
LINK_COPIES = len(PARTS) * sum(len(u) for u in STAGES) * 6


def half(rows, unit):
    tiles = rows // 8
    return 8 * ((tiles + unit % 2) // 2)


def device(x, y, z, core):
    return {"group": y % 2 * 2 + core, "fsdp": y // 2 * 16 + x * 4 + z}


def kernel(grads, params, one, two, coding, holders, out_params, out_one, out_two, out_parity, *scratch):
    bufs = [scratch[8 * p : 8 * p + 8] for p in range(len(PARTS))]
    state, results, shared, link_send, link_recv, own_sem, peer_sem, peer_send, misc = scratch[8 * len(PARTS) :]
    group, fsdp = lax.axis_index("group"), lax.axis_index("fsdp")
    core = group % 2
    here = (fsdp // 4 % 4, fsdp // 16 * 2 + group // 2, fsdp % 4)

    def along(axis, distance):
        there = list(here)
        there[axis] = (there[axis] + distance) % 4
        return device(*there, core)

    ahead = [along(axis, 1) for axis in range(3)]
    behind = [along(axis, 3) for axis in range(3)]
    other_core = device(*here, 1 - core)
    partner = device(here[0], here[1] // 2 * 2 + 1 - here[1] % 2, here[2], core)

    places = [[(here[axis] + d) % 4 for d in STEP] for axis in range(3)]
    starts = (
        [v * (4 * ROWS) for v in places[0]],
        [v // 2 * (16 * ROWS) for v in places[1]],
        [v * ROWS for v in places[2]],
    )
    group_rows = [v % 2 * 2 for v in places[1]]

    def shard_of(p, slots, which):
        order, first, rows = PARTS[p]
        slot = {axis: slots[i] for i, axis in enumerate(order)}
        start = starts[0][slot[0]] + starts[1][slot[1]] + starts[2][slot[2]] + first
        return grads.at[pl.ds(pl.multiple_of(start, 8), rows), group_rows[slot[1]] + which]

    def slots_of(unit):
        out = [()]
        for first, count in unit:
            out = [s + (i,) for s in out for i in range(first, first + count)]
        return out

    def at(ref, lead, unit, rows=None):
        index = tuple(lead) + tuple(pl.ds(first, count) for first, count in unit)
        if rows is not None:
            index += (pl.ds(rows[0], rows[1] - rows[0]),)
        return ref.at[index] if index else ref

    def number(p, u, m):
        return (p * len(UNITS) + u) * 4 + m

    def load_own(p, u):
        for m in range(4):
            for s in slots_of(UNITS[u]):
                pltpu.make_async_copy(
                    shard_of(p, (m,) + s, core), bufs[p][0].at[(m,) + s], own_sem.at[number(p, u, m)]
                ).start()

    def give_peer(p, u, slots):
        for m in slots:
            for s in slots_of(UNITS[u]):
                pltpu.make_async_remote_copy(
                    src_ref=shard_of(p, (m,) + s, 1 - core),
                    dst_ref=bufs[p][1].at[(m,) + s],
                    send_sem=peer_send.at[p],
                    recv_sem=peer_sem.at[number(p, u, m)],
                    device_id=other_core,
                    device_id_type=MESH,
                ).start()

    def arrived(ref, sem):
        pltpu.make_async_copy(ref, ref, sem).wait()

    def ready(p, u, m):
        arrived(at(bufs[p][0], (m,), UNITS[u]), own_sem.at[number(p, u, m)])
        arrived(at(bufs[p][1], (m,), UNITS[u]), peer_sem.at[number(p, u, m)])

    def add(target, terms, slots):
        for s in slots:
            total = target.at[s][...] if s else target[...]
            for term in terms:
                total = total + (term.at[s][...] if s else term[...])
            if s:
                target.at[s][...] = total
            else:
                target[...] = total

    def local(unit):
        out = [()]
        for _, count in unit:
            out = [s + (i,) for s in out for i in range(count)]
        return out

    sent = []

    def link_number(p, stage, u, which):
        before = sum(len(units) for units in STAGES[:stage]) + u
        return (p * sum(len(units) for units in STAGES) + before) * 6 + which

    def send(p, stage, u, which, source, target, to):
        i = link_number(p, stage, u, which)
        copy = pltpu.make_async_remote_copy(
            src_ref=source,
            dst_ref=target,
            send_sem=link_send.at[i],
            recv_sem=link_recv.at[i],
            device_id=to,
            device_id_type=MESH,
        )
        copy.start()
        sent.append(copy)

    def came(p, stage, u, which, ref):
        arrived(ref, link_recv.at[link_number(p, stage, u, which)])

    def views(p, stage, u):
        order, _, rows = PARTS[p]
        unit = STAGES[stage][u]
        cut = half(rows, u)
        lead = (OWN,) * stage
        first, last = (0, cut), (cut, rows)
        values = lambda m, r=None: at(bufs[p][0], lead + (m,), unit, r)
        peers = lambda m, r=None: at(bufs[p][1], lead + (m,), unit, r)
        far = lambda way: at(bufs[p][2 + 2 * stage], (way,), unit, (0, cut if way == 0 else rows - cut))
        near = lambda way, r=None: at(bufs[p][3 + 2 * stage], (way,), unit, r)
        return order[stage], first, last, values, peers, far, near, local(unit)

    def send_far(p, stage, u):
        axis, first, last, values, peers, far, near, slots = views(p, stage, u)
        if stage == 0:
            ready(p, u, FAR)
            add(values(FAR), [peers(FAR)], slots)
        send(p, stage, u, 0, values(FAR, first), far(0), ahead[axis])
        send(p, stage, u, 1, values(FAR, last), far(1), behind[axis])

    def send_near(p, stage, u):
        axis, first, last, values, peers, far, near, slots = views(p, stage, u)
        if stage == 0:
            ready(p, u, AFTER)
            add(values(AFTER, last), [peers(AFTER, last)], slots)
        send(p, stage, u, 2, values(AFTER, last), near(0, last), ahead[axis])
        if stage == 0:
            ready(p, u, BEFORE)
            add(values(BEFORE, first), [peers(BEFORE, first)], slots)
        send(p, stage, u, 3, values(BEFORE, first), near(1, first), behind[axis])

    def pass_on(p, stage, u):
        axis, first, last, values, peers, far, near, slots = views(p, stage, u)
        came(p, stage, u, 0, far(0))
        add(values(AFTER, first), ([peers(AFTER, first)] if stage == 0 else []) + [far(0)], slots)
        send(p, stage, u, 4, values(AFTER, first), near(0, first), ahead[axis])
        came(p, stage, u, 1, far(1))
        add(values(BEFORE, last), ([peers(BEFORE, last)] if stage == 0 else []) + [far(1)], slots)
        send(p, stage, u, 5, values(BEFORE, last), near(1, last), behind[axis])

    def finish(p, stage, u):
        axis, first, last, values, peers, far, near, slots = views(p, stage, u)
        if stage == 0:
            ready(p, u, OWN)
        came(p, stage, u, 2, near(0, last))
        came(p, stage, u, 3, near(1, first))
        came(p, stage, u, 4, near(0, first))
        came(p, stage, u, 5, near(1, last))
        add(values(OWN), ([peers(OWN)] if stage == 0 else []) + [near(0), near(1)], slots)

    parts = range(len(PARTS))

    def every(step, *args):
        for p in parts:
            step(p, *args)

    def load(u):
        every(load_own, u - 1)

    def give(u):
        every(give_peer, u - 1, (FAR,))
        every(give_peer, u - 1, (AFTER, BEFORE))
        every(give_peer, u - 1, (OWN,))

    def begin(stage, u):
        every(send_far, stage, u - 1)
        every(send_near, stage, u - 1)

    def far_of(stage, u):
        every(send_far, stage, u - 1)

    def near_of(stage, u):
        every(send_near, stage, u - 1)

    def dep(stage, u):
        every(pass_on, stage, u - 1)

    def done(stage, u):
        every(finish, stage, u - 1)

    load(1)
    for i, ref in enumerate((params, one, two)):
        pltpu.make_async_copy(ref, state.at[i], misc.at[i]).start()
    load(2)
    barrier = pltpu.get_barrier_semaphore()
    for to in ahead + behind + [other_core]:
        pl.semaphore_signal(barrier, inc=1, device_id=to, device_id_type=MESH)
    pl.semaphore_wait(barrier, 7)
    give(1)
    give(2)
    begin(0, 1)
    load(3), give(3)
    begin(0, 2)
    load(4), give(4)
    dep(0, 1)
    begin(0, 3)
    load(5), give(5), load(6), give(6)
    dep(0, 2)
    done(0, 1), far_of(1, 1)
    begin(0, 4)
    load(7), give(7), load(8), give(8), load(9), give(9)
    dep(0, 3)
    done(0, 2), far_of(1, 2)
    begin(0, 5)
    done(0, 3), near_of(1, 1)
    dep(0, 4)
    begin(0, 6)
    done(0, 4), near_of(1, 2)
    dep(1, 1)
    dep(0, 5)
    begin(0, 7)
    done(0, 5), far_of(1, 3)
    dep(1, 2)
    dep(0, 6)
    begin(0, 8)
    done(0, 6), done(1, 1), far_of(2, 1)
    dep(0, 7)
    begin(0, 9)
    done(0, 7), done(1, 2), near_of(2, 1)
    dep(0, 8), dep(0, 9)
    done(0, 8), near_of(1, 3)
    dep(2, 1), dep(1, 3)

    for i in range(3):
        arrived(state.at[i], misc.at[i])
    for p in parts:
        arrived(bufs[p][0], peer_send.at[p])

    copies, across, beside = [], [], []
    for p in parts:
        finish(p, 0, 8)
        finish(p, 1, 2)
        finish(p, 2, 0)
        _, start, rows = PARTS[p]
        mine = pl.ds(start, rows)
        gradient = bufs[p][0].at[OWN, OWN, OWN][...]
        values = state.at[0, mine][...]
        first_moment = 0.9 * state.at[1, mine][...] + 0.1 * gradient
        second_moment = 0.95 * state.at[2, mine][...] + 0.05 * gradient * gradient
        first_fix = 1.0 - 0.9**10
        second_fix = 1.0 - 0.95**10
        update = first_moment / first_fix / (jnp.sqrt(second_moment / second_fix) + 1e-08) + 0.1 * values
        shared.at[0, mine][...] = values - 0.05 * update
        results.at[0, mine][...] = first_moment
        results.at[1, mine][...] = second_moment
        for n, (to, slot, kept) in enumerate(((partner, 2, across), (other_core, 1, beside))):
            copy = pltpu.make_async_remote_copy(
                src_ref=shared.at[0, mine],
                dst_ref=shared.at[slot, mine],
                send_sem=misc.at[3 + 6 * p + 2 * n],
                recv_sem=misc.at[4 + 6 * p + 2 * n],
                device_id=to,
                device_id_type=MESH,
            )
            copy.start()
            kept.append(copy)
        for n, (source, target) in enumerate(
            ((shared.at[0], out_params), (results.at[0], out_one), (results.at[1], out_two))
        ):
            copy = pltpu.make_async_copy(source.at[mine], target.at[mine], misc.at[21 + 4 * p + n])
            copy.start()
            copies.append(copy)

    for copy in sent:
        copy.wait_send()

    def weight(g):
        none = jnp.float32(0.0)
        return jnp.where(holders[0, 0] == group, coding[0, g], none) + jnp.where(
            holders[0, 1] == group, coding[1, g], none
        )

    far_side = (1 - group // 2) * 2
    weights = [
        weight(group),
        weight(group // 2 * 2 + 1 - core),
        weight(far_side + core),
        weight(far_side + 1 - core),
    ]
    relays = []
    for p in parts:
        _, start, rows = PARTS[p]
        mine = pl.ds(start, rows)
        across[p].wait()
        copy = pltpu.make_async_remote_copy(
            src_ref=shared.at[2, mine],
            dst_ref=shared.at[3, mine],
            send_sem=misc.at[7 + 6 * p],
            recv_sem=misc.at[8 + 6 * p],
            device_id=other_core,
            device_id_type=MESH,
        )
        copy.start()
        relays.append(copy)
    for p in parts:
        _, start, rows = PARTS[p]
        mine = pl.ds(start, rows)
        beside[p].wait()
        relays[p].wait()
        total = weights[0] * shared.at[0, mine][...]
        for slot in range(1, 4):
            total = total + weights[slot] * shared.at[slot, mine][...]
        results.at[2, mine][...] = total
        copy = pltpu.make_async_copy(results.at[2, mine], out_parity.at[mine], misc.at[24 + 4 * p])
        copy.start()
        copies.append(copy)
    for copy in copies:
        copy.wait()


def shards(grads, params, moment_one, moment_two, coding, holders):
    rows = grads.shape[2] // LANES
    partial = grads.reshape(4, rows, LANES).transpose(1, 0, 2)
    flat = lambda t: t.reshape(ROWS, LANES)
    anywhere = pl.BlockSpec(memory_space=pltpu.HBM)
    scalars = pl.BlockSpec(memory_space=pltpu.SMEM)
    f32 = jnp.float32
    scratch = []
    for _, _, n in PARTS:
        h = max(half(n, 0), half(n, 1), n - half(n, 0))
        scratch += [
            pltpu.VMEM((4, 4, 4, n, LANES), f32),
            pltpu.VMEM((4, 4, 4, n, LANES), f32),
            pltpu.VMEM((2, 4, 4, h, LANES), f32),
            pltpu.VMEM((2, 4, 4, n, LANES), f32),
            pltpu.VMEM((2, 4, h, LANES), f32),
            pltpu.VMEM((2, 4, n, LANES), f32),
            pltpu.VMEM((2, h, LANES), f32),
            pltpu.VMEM((2, n, LANES), f32),
        ]
    scratch += [
        pltpu.VMEM((3, ROWS, LANES), f32),
        pltpu.VMEM((3, ROWS, LANES), f32),
        pltpu.VMEM((4, ROWS, LANES), f32),
        pltpu.SemaphoreType.DMA((LINK_COPIES,)),
        pltpu.SemaphoreType.DMA((LINK_COPIES,)),
        pltpu.SemaphoreType.DMA((len(PARTS) * len(UNITS) * 4,)),
        pltpu.SemaphoreType.DMA((len(PARTS) * len(UNITS) * 4,)),
        pltpu.SemaphoreType.DMA((len(PARTS),)),
        pltpu.SemaphoreType.DMA((3 + 10 * len(PARTS),)),
    ]
    out = pl.pallas_call(
        kernel,
        out_shape=[jax.ShapeDtypeStruct((ROWS, LANES), f32)] * 4,
        in_specs=[anywhere] * 4 + [scalars] * 2,
        out_specs=[anywhere] * 4,
        scratch_shapes=scratch,
        compiler_params=pltpu.CompilerParams(
            collective_id=0, has_side_effects=True, vmem_limit_bytes=60 * 1024 * 1024
        ),
    )(partial, flat(params), flat(moment_one), flat(moment_two), coding.T, holders)
    return tuple(t.reshape(1, ROWS * LANES) for t in out)


def solution(mesh):
    return jax.shard_map(
        shards,
        mesh=mesh,
        in_specs=(
            P(("group", "fsdp"), None, None),
            P("group", "fsdp"),
            P("group", "fsdp"),
            P("group", "fsdp"),
            P(),
            P("fsdp", None),
        ),
        out_specs=(P("group", "fsdp"), P("group", "fsdp"), P("group", "fsdp"), P("group", "fsdp")),
        check_vma=False,
    )
```

time: 294 us -> 70.4 us (0.24)
  waiting for transfers between devices: 254 us -> 0 us
  Pallas kernels: 0 us -> 63.3 us
  local copies, waits for them, and re-layouts: 20.4 us -> 6.27 us
  between operations: 14.1 us -> 0.64 us
  other arithmetic: 5.39 us -> 0 us
    unnamed x3 -> x0, waiting for transfers between devices: 219 us -> none
    pallas_call x0 -> x1, Pallas kernels: none -> 63.3 us  [shards(): pl.pallas_call(kernel, out_shape=[jax.ShapeDtypeStruct((ROWS, LANES), f32...]
    psum x1 -> x0, waiting for transfers between devices: 34.9 us -> none  [shards(): parity_totals = lax.psum(weighted, 'group')]
    unnamed x13 -> x4, local copies, waits for them, and re-layouts: 20.4 us -> 6.27 us
  transfers between devices with their start and end apart: 2 -> 0, of which waited for: 2 -> 0; matrix products, arithmetic and copies ran while one was open for 0% -> 0% of each run, Pallas kernels for 0% -> 0%
where the time goes in v1:
time: 70.4 us; the launch traced here: 70.2 us
  Pallas kernels  63.3 us (90%)
  local copies, waits for them, and re-layouts  6.27 us (9%)
    pallas_call x1, Pallas kernels, shards(): pl.pallas_call(kernel, out_shape=[jax.ShapeDtypeStruct((ROWS, LANES), f32...  63.3 us
    unnamed x4, local copies, waits for them, and re-layouts  6.27 us

profile of v1, /device:TPU:1, one launch (start us, length us, event | category | flops | bytes accessed | tf_op | source)
XLA Modules:
  0.0 70.2 jit_solution(12671032689804345056)
XLA Ops:
  0.6 63.3 %shard_map.93 = (f32[256,128]{1,0:T(8,128)}, f32[256,128]{1,0:T(8,128)}, f32[256,128]{1,0:T(8,128)}, f32[256,128]{1,0:T(8,128)}) custom-call(f32[8192,4,128]{2,1,0:T(4,128)} %bitcast.11, f32[256,128]{1,0:T(8,128)} %bitcast.12, f32[256,128]{1,0:T(8,128)} %bitcast.13, f32[256,128]{1,0:T(8,128)} %bitcast.14, f32[2,4]{1,0:T(2,128)} %bitcast.19, s32[1,2]{1,0:T(1,128)} %holders.1), custom_call_target="tpu_custom_call" | custom-call | tf_op jit(solution)/shard_map/pallas_call | solution.py:396
  63.9 1.6 %copy.14 = f32[1,32768]{1,0:T(1,128)} copy(f32[1,32768]{1,0:T(1,128)} %bitcast.18) | data formatting | bytes 262144
  65.5 1.6 %copy.15 = f32[1,32768]{1,0:T(1,128)} copy(f32[1,32768]{1,0:T(1,128)} %bitcast.17) | data formatting | bytes 262144
  67.0 1.6 %copy.16 = f32[1,32768]{1,0:T(1,128)} copy(f32[1,32768]{1,0:T(1,128)} %bitcast.16) | data formatting | bytes 262144
  68.6 1.6 %copy.17 = f32[1,32768]{1,0:T(1,128)} copy(f32[1,32768]{1,0:T(1,128)} %bitcast.15) | data formatting | bytes 262144

commit v2 on v1

--- a/solution.py
+++ b/solution.py
@@ -30,7 +30,25 @@
 UNITS2 = ((ONE["far"],), (ONE["near"],), (ONE["own"],))
 UNITS3 = ((),)
 STAGES = (UNITS, UNITS2, UNITS3)
-LINK_COPIES = len(PARTS) * sum(len(u) for u in STAGES) * 6
+PER_PART = sum(len(units) for units in STAGES)
+LOADS = (((0, 1), (0, 1)), ((0, 1), (1, 3)), ((1, 2), (0, 4)), ((3, 1), (0, 4)))
+LOAD_OF = (0, 1, 2, 2, 1, 3, 3, 2, 3)
+PLAN = (
+    "g1 g2 g3 b1",
+    "G1 g4 b2 G2",
+    "g5 g6 b3 G3",
+    "d1 g7 g8 b4",
+    "g9 G4 d2 o1",
+    "F1 b5 d3 o2",
+    "F2 b6 d4 o3",
+    "N1 b7 d5 D1",
+    "o4 N2 b8 d6",
+    "o5 F3 b9 d7",
+    "D2 o6 O1 f1",
+    "d8 o7 O2 n1",
+    "d9 o8 N3 e1",
+    "D3",
+)
 
 
 def half(rows, unit):
@@ -42,9 +60,9 @@
     return {"group": y % 2 * 2 + core, "fsdp": y // 2 * 16 + x * 4 + z}
 
 
-def kernel(grads, params, one, two, coding, holders, out_params, out_one, out_two, out_parity, *scratch):
+def kernel(grads, params, one, two, coding, holders, results, *scratch):
     bufs = [scratch[8 * p : 8 * p + 8] for p in range(len(PARTS))]
-    state, results, shared, link_send, link_recv, own_sem, peer_sem, peer_send, misc = scratch[8 * len(PARTS) :]
+    state, shared, link_send, link_recv, own_sem, peer_sem, peer_send, misc = scratch[8 * len(PARTS) :]
     group, fsdp = lax.axis_index("group"), lax.axis_index("fsdp")
     core = group % 2
     here = (fsdp // 4 % 4, fsdp // 16 * 2 + group // 2, fsdp % 4)
@@ -85,34 +103,47 @@
             index += (pl.ds(rows[0], rows[1] - rows[0]),)
         return ref.at[index] if index else ref
 
-    def number(p, u, m):
-        return (p * len(UNITS) + u) * 4 + m
-
-    def load_own(p, u):
+    def load_own(p, g):
         for m in range(4):
-            for s in slots_of(UNITS[u]):
+            for s in slots_of(LOADS[g]):
                 pltpu.make_async_copy(
-                    shard_of(p, (m,) + s, core), bufs[p][0].at[(m,) + s], own_sem.at[number(p, u, m)]
+                    shard_of(p, (m,) + s, core), bufs[p][0].at[(m,) + s], own_sem.at[p * len(LOADS) + g]
                 ).start()
 
-    def give_peer(p, u, slots):
+    def give_peer(p, block, slots, sem):
         for m in slots:
-            for s in slots_of(UNITS[u]):
+            for s in slots_of(block):
                 pltpu.make_async_remote_copy(
                     src_ref=shard_of(p, (m,) + s, 1 - core),
                     dst_ref=bufs[p][1].at[(m,) + s],
                     send_sem=peer_send.at[p],
-                    recv_sem=peer_sem.at[number(p, u, m)],
+                    recv_sem=sem,
                     device_id=other_core,
                     device_id_type=MESH,
                 ).start()
 
+    def sent_on(p, u):
+        return peer_sem.at[p * len(UNITS) + u]
+
+    def kept(p, g):
+        return peer_sem.at[(len(PARTS) * len(UNITS)) + p * len(LOADS) + g]
+
     def arrived(ref, sem):
         pltpu.make_async_copy(ref, ref, sem).wait()
 
+    waited = set()
+
     def ready(p, u, m):
-        arrived(at(bufs[p][0], (m,), UNITS[u]), own_sem.at[number(p, u, m)])
-        arrived(at(bufs[p][1], (m,), UNITS[u]), peer_sem.at[number(p, u, m)])
+        g, rest = LOAD_OF[u], m == OWN
+        if (p, g) not in waited:
+            waited.add((p, g))
+            arrived(at(bufs[p][0], (), ((0, 4),) + LOADS[g]), own_sem.at[p * len(LOADS) + g])
+        if rest and (p, g, OWN) not in waited:
+            waited.add((p, g, OWN))
+            arrived(at(bufs[p][1], (OWN,), LOADS[g]), kept(p, g))
+        if not rest and (p, u, FAR) not in waited:
+            waited.add((p, u, FAR))
+            arrived(at(bufs[p][1], (), ((0, 3),) + UNITS[u]), sent_on(p, u))
 
     def add(target, terms, slots):
         for s in slots:
@@ -130,27 +161,18 @@
             out = [s + (i,) for s in out for i in range(count)]
         return out
 
-    sent = []
-
-    def link_number(p, stage, u, which):
-        before = sum(len(units) for units in STAGES[:stage]) + u
-        return (p * sum(len(units) for units in STAGES) + before) * 6 + which
-
-    def send(p, stage, u, which, source, target, to):
-        i = link_number(p, stage, u, which)
-        copy = pltpu.make_async_remote_copy(
+    def landing(p, stage, u, kind):
+        return link_recv.at[(p * PER_PART + sum(len(units) for units in STAGES[:stage]) + u) * 3 + kind]
+
+    def send(p, stage, u, kind, source, target, to):
+        pltpu.make_async_remote_copy(
             src_ref=source,
             dst_ref=target,
-            send_sem=link_send.at[i],
-            recv_sem=link_recv.at[i],
+            send_sem=link_send.at[3 * p + stage],
+            recv_sem=landing(p, stage, u, kind),
             device_id=to,
             device_id_type=MESH,
-        )
-        copy.start()
-        sent.append(copy)
-
-    def came(p, stage, u, which, ref):
-        arrived(ref, link_recv.at[link_number(p, stage, u, which)])
+        ).start()
 
     def views(p, stage, u):
         order, _, rows = PARTS[p]
@@ -181,25 +203,22 @@
         if stage == 0:
             ready(p, u, BEFORE)
             add(values(BEFORE, first), [peers(BEFORE, first)], slots)
-        send(p, stage, u, 3, values(BEFORE, first), near(1, first), behind[axis])
+        send(p, stage, u, 2, values(BEFORE, first), near(1, first), behind[axis])
 
     def pass_on(p, stage, u):
         axis, first, last, values, peers, far, near, slots = views(p, stage, u)
-        came(p, stage, u, 0, far(0))
+        arrived(far(0), landing(p, stage, u, 0))
         add(values(AFTER, first), ([peers(AFTER, first)] if stage == 0 else []) + [far(0)], slots)
-        send(p, stage, u, 4, values(AFTER, first), near(0, first), ahead[axis])
-        came(p, stage, u, 1, far(1))
+        send(p, stage, u, 2, values(AFTER, first), near(0, first), ahead[axis])
+        arrived(far(1), landing(p, stage, u, 1))
         add(values(BEFORE, last), ([peers(BEFORE, last)] if stage == 0 else []) + [far(1)], slots)
-        send(p, stage, u, 5, values(BEFORE, last), near(1, last), behind[axis])
+        send(p, stage, u, 2, values(BEFORE, last), near(1, last), behind[axis])
 
     def finish(p, stage, u):
         axis, first, last, values, peers, far, near, slots = views(p, stage, u)
         if stage == 0:
             ready(p, u, OWN)
-        came(p, stage, u, 2, near(0, last))
-        came(p, stage, u, 3, near(1, first))
-        came(p, stage, u, 4, near(0, first))
-        came(p, stage, u, 5, near(1, last))
+        arrived(at(bufs[p][3 + 2 * stage], (), ((0, 2),) + STAGES[stage][u]), landing(p, stage, u, 2))
         add(values(OWN), ([peers(OWN)] if stage == 0 else []) + [near(0), near(1)], slots)
 
     parts = range(len(PARTS))
@@ -208,79 +227,55 @@
         for p in parts:
             step(p, *args)
 
-    def load(u):
-        every(load_own, u - 1)
+    def load(g):
+        every(load_own, g - 1)
 
     def give(u):
-        every(give_peer, u - 1, (FAR,))
-        every(give_peer, u - 1, (AFTER, BEFORE))
-        every(give_peer, u - 1, (OWN,))
-
-    def begin(stage, u):
-        every(send_far, stage, u - 1)
-        every(send_near, stage, u - 1)
-
-    def far_of(stage, u):
-        every(send_far, stage, u - 1)
-
-    def near_of(stage, u):
-        every(send_near, stage, u - 1)
-
-    def dep(stage, u):
-        every(pass_on, stage, u - 1)
-
-    def done(stage, u):
-        every(finish, stage, u - 1)
+        for p in parts:
+            give_peer(p, UNITS[u - 1], (FAR, AFTER, BEFORE), sent_on(p, u - 1))
+
+    def give_own(g):
+        for p in parts:
+            give_peer(p, LOADS[g - 1], (OWN,), kept(p, g - 1))
+
+    def begin(u):
+        every(send_far, 0, u - 1)
+        every(send_near, 0, u - 1)
+
+    steps = {
+        "g": give,
+        "G": give_own,
+        "b": begin,
+        "d": lambda u: every(pass_on, 0, u - 1),
+        "o": lambda u: every(finish, 0, u - 1),
+        "F": lambda u: every(send_far, 1, u - 1),
+        "N": lambda u: every(send_near, 1, u - 1),
+        "D": lambda u: every(pass_on, 1, u - 1),
+        "O": lambda u: every(finish, 1, u - 1),
+        "f": lambda u: every(send_far, 2, u - 1),
+        "n": lambda u: every(send_near, 2, u - 1),
+        "e": lambda u: every(pass_on, 2, u - 1),
+    }
 
     load(1)
+    load(2)
     for i, ref in enumerate((params, one, two)):
         pltpu.make_async_copy(ref, state.at[i], misc.at[i]).start()
-    load(2)
+    load(3)
+    load(4)
     barrier = pltpu.get_barrier_semaphore()
     for to in ahead + behind + [other_core]:
         pl.semaphore_signal(barrier, inc=1, device_id=to, device_id_type=MESH)
     pl.semaphore_wait(barrier, 7)
-    give(1)
-    give(2)
-    begin(0, 1)
-    load(3), give(3)
-    begin(0, 2)
-    load(4), give(4)
-    dep(0, 1)
-    begin(0, 3)
-    load(5), give(5), load(6), give(6)
-    dep(0, 2)
-    done(0, 1), far_of(1, 1)
-    begin(0, 4)
-    load(7), give(7), load(8), give(8), load(9), give(9)
-    dep(0, 3)
-    done(0, 2), far_of(1, 2)
-    begin(0, 5)
-    done(0, 3), near_of(1, 1)
-    dep(0, 4)
-    begin(0, 6)
-    done(0, 4), near_of(1, 2)
-    dep(1, 1)
-    dep(0, 5)
-    begin(0, 7)
-    done(0, 5), far_of(1, 3)
-    dep(1, 2)
-    dep(0, 6)
-    begin(0, 8)
-    done(0, 6), done(1, 1), far_of(2, 1)
-    dep(0, 7)
-    begin(0, 9)
-    done(0, 7), done(1, 2), near_of(2, 1)
-    dep(0, 8), dep(0, 9)
-    done(0, 8), near_of(1, 3)
-    dep(2, 1), dep(1, 3)
+    for step in " ".join(PLAN).split():
+        steps[step[0]](int(step[1]))
 
     for i in range(3):
         arrived(state.at[i], misc.at[i])
     for p in parts:
         arrived(bufs[p][0], peer_send.at[p])
 
-    copies, across, beside = [], [], []
+    across, beside = [], []
     for p in parts:
         finish(p, 0, 8)
         finish(p, 1, 2)
@@ -294,9 +289,11 @@
         first_fix = 1.0 - 0.9**10
         second_fix = 1.0 - 0.95**10
         update = first_moment / first_fix / (jnp.sqrt(second_moment / second_fix) + 1e-08) + 0.1 * values
-        shared.at[0, mine][...] = values - 0.05 * update
-        results.at[0, mine][...] = first_moment
-        results.at[1, mine][...] = second_moment
+        new_params = values - 0.05 * update
+        shared.at[0, mine][...] = new_params
+        results.at[0, mine][...] = new_params
+        results.at[1, mine][...] = first_moment
+        results.at[2, mine][...] = second_moment
         for n, (to, slot, kept) in enumerate(((partner, 2, across), (other_core, 1, beside))):
             copy = pltpu.make_async_remote_copy(
                 src_ref=shared.at[0, mine],
@@ -308,15 +305,11 @@
             )
             copy.start()
             kept.append(copy)
-        for n, (source, target) in enumerate(
-            ((shared.at[0], out_params), (results.at[0], out_one), (results.at[1], out_two))
-        ):
-            copy = pltpu.make_async_copy(source.at[mine], target.at[mine], misc.at[21 + 4 * p + n])
-            copy.start()
-            copies.append(copy)
-
-    for copy in sent:
-        copy.wait_send()
+
+    for p in parts:
+        for stage in range(3):
+            ref = at(bufs[p][0], (), ((0, 3),)) if stage == 0 else bufs[p][0].at[(pl.ds(0, 3),) + (0,) * stage]
+            arrived(ref, link_send.at[3 * p + stage])
 
     def weight(g):
         none = jnp.float32(0.0)
@@ -354,10 +347,14 @@
         total = weights[0] * shared.at[0, mine][...]
         for slot in range(1, 4):
             total = total + weights[slot] * shared.at[slot, mine][...]
-        results.at[2, mine][...] = total
-        copy = pltpu.make_async_copy(results.at[2, mine], out_parity.at[mine], misc.at[24 + 4 * p])
+        results.at[3, mine][...] = total
+
+
+def write(results, *rest):
+    outs, sems = rest[:-1], rest[-1]
+    copies = [pltpu.make_async_copy(results.at[i], out, sems.at[i]) for i, out in enumerate(outs)]
+    for copy in copies:
         copy.start()
-        copies.append(copy)
     for copy in copies:
         copy.wait()
 
@@ -384,25 +381,32 @@
         ]
     scratch += [
         pltpu.VMEM((3, ROWS, LANES), f32),
-        pltpu.VMEM((3, ROWS, LANES), f32),
         pltpu.VMEM((4, ROWS, LANES), f32),
-        pltpu.SemaphoreType.DMA((LINK_COPIES,)),
-        pltpu.SemaphoreType.DMA((LINK_COPIES,)),
-        pltpu.SemaphoreType.DMA((len(PARTS) * len(UNITS) * 4,)),
-        pltpu.SemaphoreType.DMA((len(PARTS) * len(UNITS) * 4,)),
+        pltpu.SemaphoreType.DMA((len(PARTS) * 3,)),
+        pltpu.SemaphoreType.DMA((len(PARTS) * PER_PART * 3,)),
+        pltpu.SemaphoreType.DMA((len(PARTS) * len(LOADS),)),
+        pltpu.SemaphoreType.DMA((len(PARTS) * (len(UNITS) + len(LOADS)),)),
         pltpu.SemaphoreType.DMA((len(PARTS),)),
-        pltpu.SemaphoreType.DMA((3 + 10 * len(PARTS),)),
+        pltpu.SemaphoreType.DMA((3 + 6 * len(PARTS),)),
     ]
-    out = pl.pallas_call(
+    vmem = pl.BlockSpec(memory_space=pltpu.VMEM)
+    results = pl.pallas_call(
         kernel,
-        out_shape=[jax.ShapeDtypeStruct((ROWS, LANES), f32)] * 4,
+        out_shape=pltpu.VMEM((4, ROWS, LANES), f32),
         in_specs=[anywhere] * 4 + [scalars] * 2,
-        out_specs=[anywhere] * 4,
+        out_specs=vmem,
         scratch_shapes=scratch,
         compiler_params=pltpu.CompilerParams(
-            collective_id=0, has_side_effects=True, vmem_limit_bytes=60 * 1024 * 1024
+            collective_id=0, has_side_effects=True, vmem_limit_bytes=56 * 1024 * 1024
         ),
     )(partial, flat(params), flat(moment_one), flat(moment_two), coding.T, holders)
+    out = pl.pallas_call(
+        write,
+        out_shape=[jax.ShapeDtypeStruct((ROWS, LANES), f32)] * 4,
+        in_specs=[vmem],
+        out_specs=[anywhere] * 4,
+        scratch_shapes=[pltpu.SemaphoreType.DMA((4,))],
+    )(results)
     return tuple(t.reshape(1, ROWS * LANES) for t in out)
 
 

time: 70.4 us -> 56 us (0.80)
  Pallas kernels: 63.3 us -> 54.4 us
  local copies, waits for them, and re-layouts: 6.27 us -> 0.77 us
    pallas_call x1 -> x2, Pallas kernels: 63.3 us -> 54.4 us  [the longest x1 52.6 us: shards(): pl.pallas_call(kernel, out_shape=pltpu.VMEM((4, ROWS, LANES), f32), in_sp...]
    unnamed x4 -> x2, local copies, waits for them, and re-layouts: 6.27 us -> 0.77 us
where the time goes in v2:
time: 56 us; the launch traced here: 55.9 us
  Pallas kernels  54.4 us (97%)
  local copies, waits for them, and re-layouts  0.77 us (1%)
  between operations  0.65 us (1%)
    pallas_call x1, Pallas kernels, shards(): pl.pallas_call(kernel, out_shape=pltpu.VMEM((4, ROWS, LANES), f32), in_sp...  52.6 us
    pallas_call x1, Pallas kernels, shards(): pl.pallas_call(write, out_shape=[jax.ShapeDtypeStruct((ROWS, LANES), f32)...  1.86 us

profile of v2, /device:TPU:1, one launch (start us, length us, event | category | flops | bytes accessed | tf_op | source)
XLA Modules:
  0.0 55.9 jit_solution(17887806337078960102)
XLA Ops:
  0.6 52.6 %shard_map.93.results = f32[4,256,128]{2,1,0:T(8,128)S(1)} custom-call(f32[8192,4,128]{2,1,0:T(4,128)} %bitcast.11, f32[256,128]{1,0:T(8,128)} %bitcast.12, f32[256,128]{1,0:T(8,128)} %bitcast.13, f32[256,128]{1,0:T(8,128)} %bitcast.14, f32[2,4]{1,0:T(2,128)} %bitcast.15, s32[1,2]{1,0:T(1,128)} %holders.1), custom_call_target="tpu_custom_call" | custom-call | tf_op jit(solution)/shard_map/pallas_call | solution.py:393
  53.2 0.0 copy-start
  53.2 0.8 %copy-done = f32[4,256,128]{2,1,0:T(8,128)} copy-done((f32[4,256,128]{2,1,0:T(8,128)}, f32[4,256,128]{2,1,0:T(8,128)S(1)}, u32[]{:S(2)}) %copy-start) | copy-done | bytes 524312
  54.0 1.9 %shard_map.94 = (f32[256,128]{1,0:T(8,128)}, f32[256,128]{1,0:T(8,128)}, f32[256,128]{1,0:T(8,128)}, f32[256,128]{1,0:T(8,128)}) custom-call(f32[4,256,128]{2,1,0:T(8,128)} %copy-done), custom_call_target="tpu_custom_call" | custom-call | tf_op jit(solution)/shard_map/pallas_call | solution.py:403
Async XLA Ops:
  53.2 0.8 %copy-start = (f32[4,256,128]{2,1,0:T(8,128)}, f32[4,256,128]{2,1,0:T(8,128)S(1)}, u32[]{:S(2)}) copy-start(f32[4,256,128]{2,1,0:T(8,128)S(1)} %shard_map.93.results) | copy-start | bytes 1572868

commit v3 on v0

v3 whole, which is shorter than its diff:
```python
import jax
import jax.numpy as jnp
from jax import lax
from jax.experimental import pallas as pl
from jax.experimental.pallas import tpu as pltpu
from jax.sharding import PartitionSpec as P

MESH = pl.DeviceIdType.MESH
LANES = 128
ROWS = 256
STEP = (2, 3, 1, 0)
FAR, BEFORE, AFTER, OWN = range(4)
ORDERS = ((0, 1, 2), (1, 2, 0), (2, 0, 1))
CHUNKS = ((0, (64, 64, 64)), (192, (24, 16, 24)))
ONE = {"far": (0, 1), "near": (1, 2), "own": (3, 1)}
UNITS = tuple(
    (ONE[a], ONE[b])
    for a, b in (
        ("far", "far"),
        ("far", "near"),
        ("near", "far"),
        ("near", "near"),
        ("far", "own"),
        ("own", "far"),
        ("own", "near"),
        ("near", "own"),
        ("own", "own"),
    )
)
STAGES = (UNITS, ((ONE["far"],), (ONE["near"],), (ONE["own"],)), ((),))
PER_CHUNK = sum(len(units) for units in STAGES)
LOADS = (((0, 1), (0, 1)), ((0, 1), (1, 3)), ((1, 2), (0, 4)), ((3, 1), (0, 4)))
LOAD_OF = (0, 1, 2, 2, 1, 3, 3, 2, 3)
PIECE = 64
GIVEN = 2 * len(UNITS) + len(LOADS)
PLAN = (
    "0g2 0g4 0h2 1g1",
    "0h4 0G2 0b2 0g1",
    "1h1 0G3 0b4 1l1",
    "1l2 1l3 0g3 1l4",
    "0h1 0c2 1b1 1G1",
    "1g2 0h3 0c4 0G1",
    "0b1 0g6 1h2 1c1",
    "1g3 0h6 0d2 1G2",
    "0g5 1h3 0G4 0b3",
    "1g5 0h5 0c1 0d4",
    "1G3 0g7 1h5 1g6",
    "1d1 0h7 1g4 1b2",
    "1h6 0g8 0c3 1h4",
    "1G4 0b6 1g8 0d1",
    "0h8 1c2 1g7 1h8",
    "0o2 0F2 0g9 1h7",
    "1g9 0h9 0d3 1h9",
    "1b3 0c6 0b5 1c3",
    "0o4 0N2 1o1 1F1",
    "1d2 1b5 0c5 0d6",
    "0o1 0F1 0b7 0D2",
    "0o3 0N1 1d3 0d5",
    "1c5 1b6 0c7 1o2",
    "1F2 1d5 1b4 0o6",
    "1c6 0b8 0D1 0d7",
    "1c4 1o3 1N1 1D1",
    "1b8 0o5 0F3 1d6",
    "0c8 1o5 1F3 1b7",
    "1c8 1d4 0b9 0d8",
    "0O1 0f1 0o7 0O2",
    "0n1 1c7 1b9 0c9",
    "1d8 1o6 1O1 1f1",
    "1c9 1d7 1o4 1N2",
    "1D2 0d9 0o8 0N3",
    "0D3 0e1 1d9 1o8",
    "1N3 1D3 1o7 1O2",
    "1n1 1e1 0q1 1q1",
    "0r1 1r1 0t1 1t1",
)


def device(x, y, z, core):
    return {"group": y % 2 * 2 + core, "fsdp": y // 2 * 16 + x * 4 + z}


def kernel(grads, params, one, two, coding, holders, results, *scratch):
    bufs = [scratch[8 * k : 8 * k + 8] for k in range(len(CHUNKS))]
    state, shared, codes, held, link_send, link_recv, own_sem, peer_sem, peer_send, misc = scratch[8 * len(CHUNKS) :]
    group, fsdp = lax.axis_index("group"), lax.axis_index("fsdp")
    core = group % 2
    here = (fsdp // 4 % 4, fsdp // 16 * 2 + group // 2, fsdp % 4)

    def along(axis, distance):
        there = list(here)
        there[axis] = (there[axis] + distance) % 4
        return device(*there, core)

    ahead = [along(axis, 1) for axis in range(3)]
    behind = [along(axis, 3) for axis in range(3)]
    other_core = device(*here, 1 - core)
    partner = device(here[0], here[1] // 2 * 2 + 1 - here[1] % 2, here[2], core)

    places = [[(here[axis] + d) % 4 for d in STEP] for axis in range(3)]
    starts = (
        [v * (4 * ROWS) for v in places[0]],
        [v // 2 * (16 * ROWS) for v in places[1]],
        [v * ROWS for v in places[2]],
    )
    group_rows = [v % 2 * 2 for v in places[1]]

    def parts_of(k, odd=0):
        first, sizes = CHUNKS[k]
        out, at_row = [], 0
        for order, rows in zip(ORDERS, sizes):
            cut = 8 * ((rows // 8 + odd) // 2)
            out.append((order, at_row, at_row + cut, at_row + rows, first + at_row))
            at_row += rows
        return out

    def slots_of(unit):
        out = [()]
        for first, count in unit:
            out = [s + (i,) for s in out for i in range(first, first + count)]
        return out

    def at(ref, lead, unit, rows=None):
        index = tuple(lead) + tuple(pl.ds(first, count) for first, count in unit)
        if rows is not None:
            index += (pl.ds(rows[0], rows[1] - rows[0]),)
        return ref.at[index] if index else ref

    def arrived(ref, sem):
        pltpu.make_async_copy(ref, ref, sem).wait()

    def terms(k, slots, which):
        for order, low, _, high, first in parts_of(k):
            slot = {axis: slots[i] for i, axis in enumerate(order)}
            start = starts[0][slot[0]] + starts[1][slot[1]] + starts[2][slot[2]] + first
            rows = pl.ds(pl.multiple_of(start, 8), high - low)
            yield grads.at[rows, group_rows[slot[1]] + which], slots + (pl.ds(low, high - low),)

    def load(k, g):
        for m in range(4):
            for s in slots_of(LOADS[g]):
                for source, place in terms(k, (m,) + s, core):
                    pltpu.make_async_copy(source, bufs[k][0].at[place], own_sem.at[k * len(LOADS) + g]).start()

    def give_peer(k, block, slots, sem):
        for m in slots:
            for s in slots_of(block):
                for source, place in terms(k, (m,) + s, 1 - core):
                    pltpu.make_async_remote_copy(
                        src_ref=source,
                        dst_ref=bufs[k][1].at[place],
                        send_sem=peer_send.at[k],
                        recv_sem=sem,
                        device_id=other_core,
                        device_id_type=MESH,
                    ).start()

    def given(k, kind, i):
        return peer_sem.at[k * GIVEN + kind * len(UNITS) + i]

    waited = set()

    def ready(k, u, kind):
        g = LOAD_OF[u]
        if (k, g) not in waited:
            waited.add((k, g))
            arrived(at(bufs[k][0], (), ((0, 4),) + LOADS[g]), own_sem.at[k * len(LOADS) + g])
        if kind < 2:
            slots = ((0, 1), (1, 2))[kind]
            arrived(at(bufs[k][1], (), (slots,) + UNITS[u]), given(k, kind, u))
        elif (k, g, OWN) not in waited:
            waited.add((k, g, OWN))
            arrived(at(bufs[k][1], (OWN,), LOADS[g]), given(k, 2, g))

    def add(refs):
        total = refs[0][...]
        for ref in refs[1:]:
            total = total + ref[...]
        refs[0][...] = total

    def landing(k, stage, u, kind):
        return link_recv.at[(k * PER_CHUNK + sum(len(units) for units in STAGES[:stage]) + u) * 2 + kind]

    def send(k, stage, u, kind, source, target, to):
        pltpu.make_async_remote_copy(
            src_ref=source,
            dst_ref=target,
            send_sem=link_send.at[3 * k + stage],
            recv_sem=landing(k, stage, u, kind),
            device_id=to,
            device_id_type=MESH,
        ).start()

    def values(k, stage, u, slot, rows):
        return at(bufs[k][0], (OWN,) * stage + (slot,), STAGES[stage][u], rows)

    def far(k, stage, u, rows=None):
        return at(bufs[k][2 + 2 * stage], (), STAGES[stage][u], rows)

    def near(k, stage, u, way, rows=None):
        return at(bufs[k][3 + 2 * stage], (way,), STAGES[stage][u], rows)

    def sum_up(k, stage, u, slot, rows, others):
        lead = (OWN,) * stage + (slot,)
        here_rows = (pl.ds(rows[0], rows[1] - rows[0]),)
        for s in slots_of(STAGES[stage][u]):
            refs = [bufs[k][0].at[lead + s + here_rows]]
            if stage == 0:
                refs.append(bufs[k][1].at[lead + s + here_rows])
            refs += [ref.at[extra + s + here_rows] for ref, extra in others]
            if len(refs) > 1:
                add(refs)

    def send_far(k, stage, u):
        whole = (0, sum(CHUNKS[k][1]))
        if stage == 0:
            ready(k, u, 0)
        sum_up(k, stage, u, FAR, whole, [])
        for order, low, cut, high, _ in parts_of(k, u % 2):
            axis = order[stage]
            for rows, to in (((low, cut), ahead[axis]), ((cut, high), behind[axis])):
                send(k, stage, u, 0, values(k, stage, u, FAR, rows), far(k, stage, u, rows), to)

    def send_near(k, stage, u):
        if stage == 0:
            ready(k, u, 1)
        for order, low, cut, high, _ in parts_of(k, u % 2):
            axis = order[stage]
            for slot, way, rows, to in ((AFTER, 0, (cut, high), ahead[axis]), (BEFORE, 1, (low, cut), behind[axis])):
                sum_up(k, stage, u, slot, rows, [])
                send(k, stage, u, 1, values(k, stage, u, slot, rows), near(k, stage, u, way, rows), to)

    def pass_on(k, stage, u):
        arrived(far(k, stage, u), landing(k, stage, u, 0))
        for order, low, cut, high, _ in parts_of(k, u % 2):
            axis = order[stage]
            for slot, way, rows, to in ((AFTER, 0, (low, cut), ahead[axis]), (BEFORE, 1, (cut, high), behind[axis])):
                sum_up(k, stage, u, slot, rows, [(bufs[k][2 + 2 * stage], ())])
                send(k, stage, u, 1, values(k, stage, u, slot, rows), near(k, stage, u, way, rows), to)

    def finish(k, stage, u):
        if stage == 0:
            ready(k, u, 2)
        arrived(at(bufs[k][3 + 2 * stage], (), ((0, 2),) + STAGES[stage][u]), landing(k, stage, u, 1))
        landed = bufs[k][3 + 2 * stage]
        sum_up(k, stage, u, OWN, (0, sum(CHUNKS[k][1])), [(landed, (0,)), (landed, (1,))])

    def pieces(k):
        first, rows = CHUNKS[k][0], sum(CHUNKS[k][1])
        return [(first + at_row, first // PIECE + i) for i, at_row in enumerate(range(0, rows, PIECE))]

    def share(piece, source, target, to, n):
        start, number = piece
        mine = pl.ds(start, PIECE)
        copy = pltpu.make_async_remote_copy(
            src_ref=shared.at[source, mine],
            dst_ref=shared.at[target, mine],
            send_sem=misc.at[5 + 6 * number + 2 * n],
            recv_sem=misc.at[6 + 6 * number + 2 * n],
            device_id=to,
            device_id_type=MESH,
        )
        copy.start()
        return copy

    shares = {}

    def step_params(k, _):
        finish(k, 0, 8)
        finish(k, 1, 2)
        finish(k, 2, 0)
        if "state" not in waited:
            waited.add("state")
            for i in range(3):
                arrived(state.at[i], misc.at[i])
        for piece in pieces(k):
            mine = pl.ds(piece[0], PIECE)
            gradient = bufs[k][0].at[OWN, OWN, OWN, pl.ds(piece[0] - CHUNKS[k][0], PIECE)][...]
            values = state.at[0, mine][...]
            first_moment = 0.9 * state.at[1, mine][...] + 0.1 * gradient
            second_moment = 0.95 * state.at[2, mine][...] + 0.05 * gradient * gradient
            first_fix = 1.0 - 0.9**10
            second_fix = 1.0 - 0.95**10
            update = first_moment / first_fix / (jnp.sqrt(second_moment / second_fix) + 1e-08) + 0.1 * values
            new_params = values - 0.05 * update
            shared.at[0, mine][...] = new_params
            shares[piece] = [share(piece, 0, 2, partner, 0), share(piece, 0, 1, other_core, 1)]
            results.at[0, mine][...] = new_params
            results.at[1, mine][...] = first_moment
            results.at[2, mine][...] = second_moment

    def relay(k, _):
        for piece in pieces(k):
            shares[piece][0].wait()
            shares[piece].append(share(piece, 2, 3, other_core, 2))

    def weight(g):
        none = jnp.float32(0.0)
        return jnp.where(held[0, 0] == group, codes[0, g], none) + jnp.where(held[0, 1] == group, codes[1, g], none)

    far_side = (1 - group // 2) * 2
    def weights():
        arrived(codes, misc.at[3])
        arrived(held, misc.at[4])
        return [
            weight(group),
            weight(group // 2 * 2 + 1 - core),
            weight(far_side + core),
            weight(far_side + 1 - core),
        ]

    def parity(k, _):
        if "weights" not in shares:
            shares["weights"] = weights()
        by_slot = shares["weights"]
        for piece in pieces(k):
            shares[piece][1].wait()
            mine = pl.ds(piece[0], PIECE)
            total = by_slot[0] * shared.at[0, mine][...]
            for slot in range(1, 3):
                total = total + by_slot[slot] * shared.at[slot, mine][...]
            shares[piece][2].wait()
            results.at[3, mine][...] = total + by_slot[3] * shared.at[3, mine][...]

    steps = {
        "l": load,
        "g": lambda k, u: give_peer(k, UNITS[u], (FAR,), given(k, 0, u)),
        "h": lambda k, u: give_peer(k, UNITS[u], (AFTER, BEFORE), given(k, 1, u)),
        "G": lambda k, g: give_peer(k, LOADS[g], (OWN,), given(k, 2, g)),
        "b": lambda k, u: send_far(k, 0, u),
        "c": lambda k, u: send_near(k, 0, u),
        "d": lambda k, u: pass_on(k, 0, u),
        "o": lambda k, u: finish(k, 0, u),
        "F": lambda k, u: send_far(k, 1, u),
        "N": lambda k, u: send_near(k, 1, u),
        "D": lambda k, u: pass_on(k, 1, u),
        "O": lambda k, u: finish(k, 1, u),
        "f": lambda k, u: send_far(k, 2, u),
        "n": lambda k, u: send_near(k, 2, u),
        "e": lambda k, u: pass_on(k, 2, u),
        "q": step_params,
        "r": relay,
        "t": parity,
    }

    barrier = pltpu.get_barrier_semaphore()
    for to in ahead + behind + [other_core]:
        pl.semaphore_signal(barrier, inc=1, device_id=to, device_id_type=MESH)
    for g in range(4):
        load(0, g)
    for i, ref in enumerate((params, one, two)):
        pltpu.make_async_copy(ref, state.at[i], misc.at[i]).start()
    pltpu.make_async_copy(coding, codes, misc.at[3]).start()
    pltpu.make_async_copy(holders, held, misc.at[4]).start()
    pl.semaphore_wait(barrier, 7)
    plan = " ".join(PLAN).split()
    for step in plan:
        if step[1] == "t" and step == [s for s in plan if s[1] == "t"][-1]:
            for k in range(len(CHUNKS)):
                arrived(bufs[k][0], peer_send.at[k])
                arrived(bufs[k][0].at[pl.ds(0, 3)], link_send.at[3 * k])
                arrived(bufs[k][0].at[pl.ds(0, 3), 0], link_send.at[3 * k + 1])
                arrived(bufs[k][0].at[pl.ds(0, 3), 0, 0], link_send.at[3 * k + 2])
        steps[step[1]](int(step[0]), int(step[2]) - 1)


def write(results, *rest):
    outs, sems = rest[:-1], rest[-1]
    copies = [pltpu.make_async_copy(results.at[i], out, sems.at[i]) for i, out in enumerate(outs)]
    for copy in copies:
        copy.start()
    for copy in copies:
        copy.wait()


def shards(grads, params, moment_one, moment_two, coding, holders):
    rows = grads.shape[2] // LANES
    partial = grads.reshape(4, rows, LANES).transpose(1, 0, 2)
    flat = lambda t: t.reshape(ROWS, LANES)
    anywhere = pl.BlockSpec(memory_space=pltpu.HBM)
    vmem = pl.BlockSpec(memory_space=pltpu.VMEM)
    f32 = jnp.float32
    scratch = []
    for _, sizes in CHUNKS:
        n = sum(sizes)
        for lead in ((4, 4, 4), (4, 4, 4), (4, 4), (2, 4, 4), (4,), (2, 4), (), (2,)):
            scratch.append(pltpu.VMEM(lead + (n, LANES), f32))
    chunks = len(CHUNKS)
    scratch += [
        pltpu.VMEM((3, ROWS, LANES), f32),
        pltpu.VMEM((4, ROWS, LANES), f32),
        pltpu.SMEM((2, 4), f32),
        pltpu.SMEM((1, 2), jnp.int32),
        pltpu.SemaphoreType.DMA((chunks * 3,)),
        pltpu.SemaphoreType.DMA((chunks * PER_CHUNK * 2,)),
        pltpu.SemaphoreType.DMA((chunks * len(LOADS),)),
        pltpu.SemaphoreType.DMA((chunks * GIVEN,)),
        pltpu.SemaphoreType.DMA((chunks,)),
        pltpu.SemaphoreType.DMA((5 + 6 * (ROWS // PIECE),)),
    ]
    results = pl.pallas_call(
        kernel,
        out_shape=pltpu.VMEM((4, ROWS, LANES), f32),
        in_specs=[anywhere] * 6,
        out_specs=vmem,
        scratch_shapes=scratch,
        compiler_params=pltpu.CompilerParams(
            collective_id=0, has_side_effects=True, vmem_limit_bytes=56 * 1024 * 1024
        ),
    )(partial, flat(params), flat(moment_one), flat(moment_two), coding.T, holders)
    out = pl.pallas_call(
        write,
        out_shape=[jax.ShapeDtypeStruct((ROWS, LANES), f32)] * 4,
        in_specs=[vmem],
        out_specs=[anywhere] * 4,
        scratch_shapes=[pltpu.SemaphoreType.DMA((4,))],
    )(pltpu.with_memory_space_constraint(results, pltpu.VMEM))
    return tuple(t.reshape(1, ROWS * LANES) for t in out)


def solution(mesh):
    return jax.shard_map(
        shards,
        mesh=mesh,
        in_specs=(
            P(("group", "fsdp"), None, None),
            P("group", "fsdp"),
            P("group", "fsdp"),
            P("group", "fsdp"),
            P(),
            P("fsdp", None),
        ),
        out_specs=(P("group", "fsdp"), P("group", "fsdp"), P("group", "fsdp"), P("group", "fsdp")),
        check_vma=False,
    )
```

time: 294 us -> 49.6 us (0.17)
  waiting for transfers between devices: 254 us -> 0 us
  Pallas kernels: 0 us -> 48.8 us
  local copies, waits for them, and re-layouts: 20.4 us -> 0 us
  between operations: 14.1 us -> 0.64 us
  other arithmetic: 5.39 us -> 0 us
    unnamed x3 -> x0, waiting for transfers between devices: 219 us -> none
    pallas_call x0 -> x2, Pallas kernels: none -> 48.8 us  [the longest x1 47.9 us: shards(): pl.pallas_call(kernel, out_shape=pltpu.VMEM((4, ROWS, LANES), f32), in_sp...]
    psum x1 -> x0, waiting for transfers between devices: 34.9 us -> none  [shards(): parity_totals = lax.psum(weighted, 'group')]
    unnamed x13 -> x0, local copies, waits for them, and re-layouts: 20.4 us -> none
  transfers between devices with their start and end apart: 2 -> 0, of which waited for: 2 -> 0; matrix products, arithmetic and copies ran while one was open for 0% -> 0% of each run, Pallas kernels for 0% -> 0%
where the time goes in v3:
time: 49.6 us; the launch traced here: 49.4 us
  Pallas kernels  48.8 us (98%)
  between operations  0.64 us (1%)
    pallas_call x1, Pallas kernels, shards(): pl.pallas_call(kernel, out_shape=pltpu.VMEM((4, ROWS, LANES), f32), in_sp...  47.9 us

profile of v3, /device:TPU:1, one launch (start us, length us, event | category | flops | bytes accessed | tf_op | source)
XLA Modules:
  0.0 49.4 jit_solution(13598047703052433714)
XLA Ops:
  0.6 47.9 %shard_map.93.results = f32[4,256,128]{2,1,0:T(8,128)S(1)} custom-call(f32[8192,4,128]{2,1,0:T(4,128)} %bitcast.11, f32[256,128]{1,0:T(8,128)} %bitcast.12, f32[256,128]{1,0:T(8,128)} %bitcast.13, f32[256,128]{1,0:T(8,128)} %bitcast.14, f32[2,4]{1,0:T(2,128)} %bitcast.15, s32[1,2]{1,0:T(1,128)} %holders.1), custom_call_target="tpu_custom_call" | custom-call | tf_op jit(solution)/shard_map/pallas_call | solution.py:400
  48.6 0.8 %shard_map.94 = (f32[256,128]{1,0:T(8,128)}, f32[256,128]{1,0:T(8,128)}, f32[256,128]{1,0:T(8,128)}, f32[256,128]{1,0:T(8,128)}) custom-call(f32[4,256,128]{2,1,0:T(8,128)S(1)} %shard_map.93.results), custom_call_target="tpu_custom_call" | custom-call | tf_op jit(solution)/shard_map/pallas_call | solution.py:410

commit v4 on v3

v4 whole, which is shorter than its diff:
```python
import jax
import jax.numpy as jnp
from jax import lax
from jax.experimental import pallas as pl
from jax.experimental.pallas import tpu as pltpu
from jax.sharding import PartitionSpec as P

MESH = pl.DeviceIdType.MESH
LANES = 128
ROWS = 256
STEP = (2, 3, 1, 0)
FAR, BEFORE, AFTER, OWN = range(4)
ORDERS = ((0, 1, 2), (1, 2, 0), (2, 0, 1))
HALF = ROWS // 2
CHUNKS = ((0, (64, 64, 64)), (96, (24, 16, 24)))
FINE = (
    ((0, 1), (0, 1)),
    ((0, 1), (1, 2)),
    ((1, 2), (0, 1)),
    ((1, 2), (1, 2)),
    ((0, 1), (3, 1)),
    ((3, 1), (0, 1)),
    ((3, 1), (1, 2)),
    ((1, 2), (3, 1)),
    ((3, 1), (3, 1)),
)
COARSE = (((0, 3), (0, 3)), ((0, 3), (3, 1)), ((3, 1), (0, 3)), ((3, 1), (3, 1)))
UNITS = (FINE, COARSE,)
RANGES = tuple((((0, 1),), ((1, 2),), ((3, 1),)) if units is FINE else (((0, 3),), ((3, 1),)) for units in UNITS)
STAGES = tuple((units, ranges, ((),)) for units, ranges in zip(UNITS, RANGES))
LOADS = (
    (((0, 1), (0, 1)), ((0, 1), (1, 3)), ((1, 2), (0, 4)), ((3, 1), (0, 4))),
    (((0, 4), (0, 4)),),
)


def load_of(k, u):
    inside = lambda small, big: all(b[0] <= s[0] and s[0] + s[1] <= b[0] + b[1] for s, b in zip(small, big))
    return [inside(UNITS[k][u], group) for group in LOADS[k]].index(True)


LANDINGS = [2 * sum(len(units) for units in stages) for stages in STAGES]
GIVEN = [2 * len(units) + len(loads) for units, loads in zip(UNITS, LOADS)]
LOADED = [len(loads) for loads in LOADS]
PLAN = (
    "0g2 0g4 0g1 0h2",
    "1g1 0h4 0b2 0G2",
    "0b4 1l1 0g6 0h1",
    "0G3 0b1 0c2 1b1",
    "0g3 1h1 0c4 0G1",
    "0d2 1g3 0h6 1G1",
    "0g5 0b6 0d4 0h3",
    "0G4 1g2 1h3 0g8",
    "0c1 0d1 0h5 0g7",
    "0b3 1h2 1g4 0h8",
    "1c1 1d1 0g9 0h7",
    "1h4 0h9 0o2 0F2",
    "1b3 0o4 0N2 0o1",
    "0F1 0c6 0d6 0b5",
    "0c3 0d3 1o1 1F1",
    "1N1 0D2 1b2 1c3",
    "1d3 0b8 0o6 0c5",
    "0d5 0b7 0o3 0N1",
    "0D1 1D1 1c2 1b4",
    "0c8 1d2 1o3 0b9",
    "0c7 0d8 0o5 0F3",
    "0d7 0O1 0f1 1O1",
    "1f1 1n1 1c4 1d4",
    "0c9 1o2 1F2 1N2",
    "0d9 0o8 0N3 0D3",
    "0o7 0O2 0n1 0e1",
    "1e1 1D2 0q1 1q1",
    "1t1 0t1",
)


def device(x, y, z, core):
    return {"group": y % 2 * 2 + core, "fsdp": y // 2 * 16 + x * 4 + z}


def kernel(grads, params, one, two, coding, holders, results, *scratch):
    bufs = [scratch[12 * k : 12 * k + 12] for k in range(len(CHUNKS))]
    state, codes, held, link_send, link_recv, own_sem, peer_sem, peer_send, misc = scratch[12 * len(CHUNKS) :]
    group, fsdp = lax.axis_index("group"), lax.axis_index("fsdp")
    core = group % 2
    here = (fsdp // 4 % 4, fsdp // 16 * 2 + group // 2, fsdp % 4)

    def along(axis, distance):
        there = list(here)
        there[axis] = (there[axis] + distance) % 4
        return device(*there, core)

    ahead = [along(axis, 1) for axis in range(3)]
    behind = [along(axis, 3) for axis in range(3)]
    other_core = device(*here, 1 - core)
    across = [device(here[0], here[1] // 2 * 2 + 1 - here[1] % 2, here[2], c) for c in range(2)]
    across_other = device(here[0], here[1] // 2 * 2 + 1 - here[1] % 2, here[2], 1 - core)

    places = [[(here[axis] + d) % 4 for d in STEP] for axis in range(3)]
    starts = (
        [v * (4 * ROWS) for v in places[0]],
        [v // 2 * (16 * ROWS) for v in places[1]],
        [v * ROWS for v in places[2]],
    )
    group_rows = [v % 2 * 2 for v in places[1]]

    def parts_of(k, odd=0):
        first, sizes = CHUNKS[k]
        out, at_row = [], 0
        for order, rows in zip(ORDERS, sizes):
            cut = 8 * ((rows // 8 + odd) // 2)
            out.append((order, at_row, at_row + cut, at_row + rows, first + at_row))
            at_row += rows
        return out

    def slots_of(unit):
        out = [()]
        for first, count in unit:
            out = [s + (i,) for s in out for i in range(first, first + count)]
        return out

    def at(ref, lead, unit, rows=None):
        index = tuple(lead) + tuple(pl.ds(first, count) for first, count in unit)
        if rows is not None:
            index += (pl.ds(rows[0], rows[1] - rows[0]),)
        return ref.at[index] if index else ref

    def arrived(ref, sem):
        pltpu.make_async_copy(ref, ref, sem).wait()

    def terms(k, slots, which):
        each = sum(CHUNKS[k][1]) // 2
        for order, low, _, high, first in parts_of(k):
            slot = {axis: slots[i] for i, axis in enumerate(order)}
            start = starts[0][slot[0]] + starts[1][slot[1]] + starts[2][slot[2]] + which * HALF + CHUNKS[k][0]
            for g in range(2):
                begin, end = max(low, g * each), min(high, (g + 1) * each)
                if begin < end:
                    rows = pl.ds(pl.multiple_of(start + (begin - g * each), 8), end - begin)
                    yield grads.at[rows, group_rows[slot[1]] + g], slots + (pl.ds(begin, end - begin),)

    def load(k, g):
        for m in range(4):
            for s in slots_of(LOADS[k][g]):
                for source, place in terms(k, (m,) + s, core):
                    pltpu.make_async_copy(source, bufs[k][0].at[place], own_sem.at[sum(LOADED[:k]) + g]).start()

    def give_peer(k, block, slots, sem):
        for m in slots:
            for s in slots_of(block):
                for source, place in terms(k, (m,) + s, 1 - core):
                    pltpu.make_async_remote_copy(
                        src_ref=source,
                        dst_ref=bufs[k][1].at[place],
                        send_sem=peer_send.at[k],
                        recv_sem=sem,
                        device_id=other_core,
                        device_id_type=MESH,
                    ).start()

    def given(k, kind, i):
        return peer_sem.at[sum(GIVEN[:k]) + kind * len(UNITS[k]) + i]

    waited = set()

    def ready(k, u, kind):
        g = load_of(k, u)
        if (k, g) not in waited:
            waited.add((k, g))
            arrived(at(bufs[k][0], (), ((0, 4),) + LOADS[k][g]), own_sem.at[sum(LOADED[:k]) + g])
        if kind < 2:
            slots = ((0, 1), (1, 2))[kind]
            arrived(at(bufs[k][1], (), (slots,) + UNITS[k][u]), given(k, kind, u))
        elif (k, g, OWN) not in waited:
            waited.add((k, g, OWN))
            arrived(at(bufs[k][1], (OWN,), LOADS[k][g]), given(k, 2, g))

    def add(refs):
        total = refs[0][...]
        for ref in refs[1:]:
            total = total + ref[...]
        refs[0][...] = total

    def landing(k, stage, u, kind):
        return link_recv.at[sum(LANDINGS[:k]) + 2 * (sum(len(units) for units in STAGES[k][:stage]) + u) + kind]

    def send(k, stage, u, kind, source, target, to):
        pltpu.make_async_remote_copy(
            src_ref=source,
            dst_ref=target,
            send_sem=link_send.at[3 * k + stage],
            recv_sem=landing(k, stage, u, kind),
            device_id=to,
            device_id_type=MESH,
        ).start()

    def values(k, stage, u, slot, rows):
        return at(bufs[k][0], (OWN,) * stage + (slot,), STAGES[k][stage][u], rows)

    def far(k, stage, u, rows=None):
        return at(bufs[k][2 + 2 * stage], (), STAGES[k][stage][u], rows)

    def near(k, stage, u, way, rows=None):
        return at(bufs[k][3 + 2 * stage], (way,), STAGES[k][stage][u], rows)

    def sum_up(k, stage, u, slot, rows, others):
        lead = (OWN,) * stage + (slot,)
        here_rows = (pl.ds(rows[0], rows[1] - rows[0]),)
        for s in slots_of(STAGES[k][stage][u]):
            refs = [bufs[k][0].at[lead + s + here_rows]]
            if stage == 0:
                refs.append(bufs[k][1].at[lead + s + here_rows])
            refs += [ref.at[extra + s + here_rows] for ref, extra in others]
            if len(refs) > 1:
                add(refs)

    def send_far(k, stage, u):
        whole = (0, sum(CHUNKS[k][1]))
        if stage == 0:
            ready(k, u, 0)
        sum_up(k, stage, u, FAR, whole, [])
        for order, low, cut, high, _ in parts_of(k, u % 2):
            axis = order[stage]
            for rows, to in (((low, cut), ahead[axis]), ((cut, high), behind[axis])):
                send(k, stage, u, 0, values(k, stage, u, FAR, rows), far(k, stage, u, rows), to)

    def send_near(k, stage, u):
        if stage == 0:
            ready(k, u, 1)
        for order, low, cut, high, _ in parts_of(k, u % 2):
            axis = order[stage]
            for slot, way, rows, to in ((AFTER, 0, (cut, high), ahead[axis]), (BEFORE, 1, (low, cut), behind[axis])):
                sum_up(k, stage, u, slot, rows, [])
                send(k, stage, u, 1, values(k, stage, u, slot, rows), near(k, stage, u, way, rows), to)

    def pass_on(k, stage, u):
        arrived(far(k, stage, u), landing(k, stage, u, 0))
        for order, low, cut, high, _ in parts_of(k, u % 2):
            axis = order[stage]
            for slot, way, rows, to in ((AFTER, 0, (low, cut), ahead[axis]), (BEFORE, 1, (cut, high), behind[axis])):
                sum_up(k, stage, u, slot, rows, [(bufs[k][2 + 2 * stage], ())])
                send(k, stage, u, 1, values(k, stage, u, slot, rows), near(k, stage, u, way, rows), to)

    def finish(k, stage, u):
        if stage == 0:
            ready(k, u, 2)
        arrived(at(bufs[k][3 + 2 * stage], (), ((0, 2),) + STAGES[k][stage][u]), landing(k, stage, u, 1))
        landed = bufs[k][3 + 2 * stage]
        sum_up(k, stage, u, OWN, (0, sum(CHUNKS[k][1])), [(landed, (0,)), (landed, (1,))])

    def weights():
        arrived(codes, misc.at[2])
        arrived(held, misc.at[3])
        none = jnp.float32(0.0)
        first = group // 2 * 2
        opposite = 2 - first
        return [
            [
                jnp.where(held[0, 0] == d, codes[0, first + g], none)
                + jnp.where(held[0, 1] == d, codes[1, first + g], none)
                for g in range(2)
            ]
            for d in (group, first + 1 - core, opposite, opposite + 1)
        ]

    known = {}

    def push(k, source, target, kind, to):
        pltpu.make_async_remote_copy(
            src_ref=source,
            dst_ref=target,
            send_sem=misc.at[4 + 3 * k],
            recv_sem=misc.at[5 + 3 * k + kind],
            device_id=to,
            device_id_type=MESH,
        ).start()

    def step_params(k, _):
        if not known:
            for g, sem in ((core, misc.at[0]), (1 - core, misc.at[1])):
                arrived(state.at[g], sem)
            known["weights"] = weights()
        finish(k, 0, len(UNITS[k]) - 1)
        finish(k, 1, len(RANGES[k]) - 1)
        finish(k, 2, 0)
        new, sums, beside, landed = bufs[k][8:]
        each = sum(CHUNKS[k][1]) // 2
        mine = pl.ds(CHUNKS[k][0], each)
        first_fix = 1.0 - 0.9**10
        second_fix = 1.0 - 0.95**10
        new_params = []
        for g in range(2):
            gradient = bufs[k][0].at[OWN, OWN, OWN, pl.ds(g * each, each)][...]
            values = state.at[g, 0, mine][...]
            first_moment = 0.9 * state.at[g, 1, mine][...] + 0.1 * gradient
            second_moment = 0.95 * state.at[g, 2, mine][...] + 0.05 * gradient * gradient
            update = first_moment / first_fix / (jnp.sqrt(second_moment / second_fix) + 1e-08) + 0.1 * values
            new_params.append(values - 0.05 * update)
            new.at[g, 0][...] = new_params[g]
            new.at[g, 1][...] = first_moment
            new.at[g, 2][...] = second_moment
        total = lambda w: w[0] * new_params[0] + w[1] * new_params[1]
        by_device = known["weights"]
        for c in range(2):
            sums.at[2 + c][...] = total(by_device[2 + c])
            push(k, sums.at[2 + c], landed.at[core], 1, across[c])
        sums.at[1][...] = total(by_device[1])
        push(k, sums.at[1], beside.at[3], 0, other_core)
        push(k, new.at[1 - core], beside.at[pl.ds(0, 3)], 0, other_core)
        sums.at[0][...] = total(by_device[0])
        place = rows_in(k, core)
        for i in range(3):
            results.at[i, place][...] = new.at[core, i][...]

    def rows_in(k, which):
        return pl.ds(pl.multiple_of(which * HALF + CHUNKS[k][0], 8), sum(CHUNKS[k][1]) // 2)

    def parity(k, _):
        new, sums, beside, landed = bufs[k][8:]
        arrived(beside, misc.at[5 + 3 * k])
        place, other = rows_in(k, core), rows_in(k, 1 - core)
        for i in range(3):
            results.at[i, other][...] = beside.at[i][...]
        arrived(landed, misc.at[6 + 3 * k])
        results.at[3, place][...] = sums.at[0][...] + landed.at[core][...]
        results.at[3, other][...] = beside.at[3][...] + landed.at[1 - core][...]

    steps = {
        "l": load,
        "g": lambda k, u: give_peer(k, UNITS[k][u], (FAR,), given(k, 0, u)),
        "h": lambda k, u: give_peer(k, UNITS[k][u], (AFTER, BEFORE), given(k, 1, u)),
        "G": lambda k, g: give_peer(k, LOADS[k][g], (OWN,), given(k, 2, g)),
        "b": lambda k, u: send_far(k, 0, u),
        "c": lambda k, u: send_near(k, 0, u),
        "d": lambda k, u: pass_on(k, 0, u),
        "o": lambda k, u: finish(k, 0, u),
        "F": lambda k, u: send_far(k, 1, u),
        "N": lambda k, u: send_near(k, 1, u),
        "D": lambda k, u: pass_on(k, 1, u),
        "O": lambda k, u: finish(k, 1, u),
        "f": lambda k, u: send_far(k, 2, u),
        "n": lambda k, u: send_near(k, 2, u),
        "e": lambda k, u: pass_on(k, 2, u),
        "q": step_params,
        "t": parity,
    }

    barrier = pltpu.get_barrier_semaphore()
    for to in ahead + behind + [other_core, across_other]:
        pl.semaphore_signal(barrier, inc=1, device_id=to, device_id_type=MESH)
    for g in range(len(LOADS[0])):
        load(0, g)
    own_half, other_half = (pl.ds(pl.multiple_of(c * HALF, 8), HALF) for c in (core, 1 - core))
    for i, ref in enumerate((params, one, two)):
        pltpu.make_async_copy(ref.at[own_half], state.at[core, i], misc.at[0]).start()
    pltpu.make_async_copy(coding, codes, misc.at[2]).start()
    pltpu.make_async_copy(holders, held, misc.at[3]).start()
    pl.semaphore_wait(barrier, 8)
    plan = " ".join(PLAN).split()
    early = 12
    for number, step in enumerate(plan):
        if number == early:
            for i, ref in enumerate((params, one, two)):
                pltpu.make_async_remote_copy(
                    src_ref=ref.at[other_half],
                    dst_ref=state.at[core, i],
                    send_sem=misc.at[4 + 3 * len(CHUNKS)],
                    recv_sem=misc.at[1],
                    device_id=other_core,
                    device_id_type=MESH,
                ).start()
        if step[1] == "t" and step == [s for s in plan if s[1] == "t"][-1]:
            arrived(state.at[0], misc.at[4 + 3 * len(CHUNKS)])
            for k in range(len(CHUNKS)):
                arrived(bufs[k][0], peer_send.at[k])
                arrived(bufs[k][0].at[pl.ds(0, 3)], link_send.at[3 * k])
                arrived(bufs[k][0].at[pl.ds(0, 3), 0], link_send.at[3 * k + 1])
                arrived(bufs[k][0].at[pl.ds(0, 3), 0, 0], link_send.at[3 * k + 2])
        steps[step[1]](int(step[0]), int(step[2]) - 1)
    for k in range(len(CHUNKS)):
        arrived(bufs[k][8], misc.at[4 + 3 * k])


def write(results, *rest):
    outs, sems = rest[:-1], rest[-1]
    copies = [pltpu.make_async_copy(results.at[i], out, sems.at[i]) for i, out in enumerate(outs)]
    for copy in copies:
        copy.start()
    for copy in copies:
        copy.wait()


def shards(grads, params, moment_one, moment_two, coding, holders):
    rows = grads.shape[2] // LANES
    partial = grads.reshape(4, rows, LANES).transpose(1, 0, 2)
    flat = lambda t: t.reshape(ROWS, LANES)
    anywhere = pl.BlockSpec(memory_space=pltpu.HBM)
    vmem = pl.BlockSpec(memory_space=pltpu.VMEM)
    f32 = jnp.float32
    scratch = []
    for _, sizes in CHUNKS:
        n = sum(sizes)
        for lead in ((4, 4, 4), (4, 4, 4), (4, 4), (2, 4, 4), (4,), (2, 4), (), (2,)):
            scratch.append(pltpu.VMEM(lead + (n, LANES), f32))
        for lead in ((2, 3), (4,), (4,), (2,)):
            scratch.append(pltpu.VMEM(lead + (n // 2, LANES), f32))
    chunks = len(CHUNKS)
    scratch += [
        pltpu.VMEM((2, 3, HALF, LANES), f32),
        pltpu.SMEM((2, 4), f32),
        pltpu.SMEM((1, 2), jnp.int32),
        pltpu.SemaphoreType.DMA((chunks * 3,)),
        pltpu.SemaphoreType.DMA((sum(LANDINGS),)),
        pltpu.SemaphoreType.DMA((sum(LOADED),)),
        pltpu.SemaphoreType.DMA((sum(GIVEN),)),
        pltpu.SemaphoreType.DMA((chunks,)),
        pltpu.SemaphoreType.DMA((5 + 3 * chunks,)),
    ]
    results = pl.pallas_call(
        kernel,
        out_shape=pltpu.VMEM((4, ROWS, LANES), f32),
        in_specs=[anywhere] * 6,
        out_specs=vmem,
        scratch_shapes=scratch,
        compiler_params=pltpu.CompilerParams(
            collective_id=0, has_side_effects=True, vmem_limit_bytes=56 * 1024 * 1024
        ),
    )(partial, flat(params), flat(moment_one), flat(moment_two), coding.T, holders)
    out = pl.pallas_call(
        write,
        out_shape=[jax.ShapeDtypeStruct((ROWS, LANES), f32)] * 4,
        in_specs=[vmem],
        out_specs=[anywhere] * 4,
        scratch_shapes=[pltpu.SemaphoreType.DMA((4,))],
    )(pltpu.with_memory_space_constraint(results, pltpu.VMEM))
    return tuple(t.reshape(1, ROWS * LANES) for t in out)


def solution(mesh):
    return jax.shard_map(
        shards,
        mesh=mesh,
        in_specs=(
            P(("group", "fsdp"), None, None),
            P("group", "fsdp"),
            P("group", "fsdp"),
            P("group", "fsdp"),
            P(),
            P("fsdp", None),
        ),
        out_specs=(P("group", "fsdp"), P("group", "fsdp"), P("group", "fsdp"), P("group", "fsdp")),
        check_vma=False,
    )
```

time: 49.6 us -> 48 us (0.968)
  Pallas kernels: 48.8 us -> 47.2 us
    pallas_call x1, Pallas kernels: 47.9 us -> 46.4 us  [shards(): pl.pallas_call(kernel, out_shape=pltpu.VMEM((4, ROWS, LANES), f32), in_sp...]
where the time goes in v4:
time: 48 us; the launch traced here: 47.8 us
  Pallas kernels  47.2 us (98%)
  between operations  0.64 us (1%)
    pallas_call x1, Pallas kernels, shards(): pl.pallas_call(kernel, out_shape=pltpu.VMEM((4, ROWS, LANES), f32), in_sp...  46.4 us

profile of v4, /device:TPU:1, one launch (start us, length us, event | category | flops | bytes accessed | tf_op | source)
XLA Modules:
  0.0 47.8 jit_solution(1284813130450167008)
XLA Ops:
  0.6 46.4 %shard_map.93.results = f32[4,256,128]{2,1,0:T(8,128)S(1)} custom-call(f32[8192,4,128]{2,1,0:T(4,128)} %bitcast.11, f32[256,128]{1,0:T(8,128)} %bitcast.12, f32[256,128]{1,0:T(8,128)} %bitcast.13, f32[256,128]{1,0:T(8,128)} %bitcast.14, f32[2,4]{1,0:T(2,128)} %bitcast.15, s32[1,2]{1,0:T(1,128)} %holders.1), custom_call_target="tpu_custom_call" | custom-call | tf_op jit(solution)/shard_map/pallas_call | solution.py:419
  47.0 0.8 %shard_map.94 = (f32[256,128]{1,0:T(8,128)}, f32[256,128]{1,0:T(8,128)}, f32[256,128]{1,0:T(8,128)}, f32[256,128]{1,0:T(8,128)}) custom-call(f32[4,256,128]{2,1,0:T(8,128)S(1)} %shard_map.93.results), custom_call_target="tpu_custom_call" | custom-call | tf_op jit(solution)/shard_map/pallas_call | solution.py:429

commit v5 on v4

--- a/solution.py
+++ b/solution.py
@@ -10,9 +10,9 @@
 ROWS = 256
 STEP = (2, 3, 1, 0)
 FAR, BEFORE, AFTER, OWN = range(4)
-ORDERS = ((0, 1, 2), (1, 2, 0), (2, 0, 1))
+ORDERS = ((0, 1, 2), (1, 2, 0), (2, 0, 1), (2, 1, 0))
 HALF = ROWS // 2
-CHUNKS = ((0, (64, 64, 64)), (96, (24, 16, 24)))
+CHUNKS = ((0, (64, 64, 48, 16)), (96, (24, 16, 16, 8)))
 FINE = (
     ((0, 1), (0, 1)),
     ((0, 1), (1, 2)),
@@ -42,14 +42,15 @@
 LANDINGS = [2 * sum(len(units) for units in stages) for stages in STAGES]
 GIVEN = [2 * len(units) + len(loads) for units, loads in zip(UNITS, LOADS)]
 LOADED = [len(loads) for loads in LOADS]
+RAW = (0, 1)
 PLAN = (
-    "0g2 0g4 0g1 0h2",
-    "1g1 0h4 0b2 0G2",
-    "0b4 1l1 0g6 0h1",
-    "0G3 0b1 0c2 1b1",
-    "0g3 1h1 0c4 0G1",
-    "0d2 1g3 0h6 1G1",
-    "0g5 0b6 0d4 0h3",
+    "0b2 0g4 0g1 0h2",
+    "1g1 0h4 0G2 0b4",
+    "1l1 0g6 0h1 0G3",
+    "0b1 0c2 1b1 0g3",
+    "1h1 0c4 0G1 0x2",
+    "1g3 0h6 1G1 0g5",
+    "0b6 0d4 0d2 0h3",
     "0G4 1g2 1h3 0g8",
     "0c1 0d1 0h5 0g7",
     "0b3 1h2 1g4 0h8",
@@ -80,7 +81,7 @@
 
 def kernel(grads, params, one, two, coding, holders, results, *scratch):
     bufs = [scratch[12 * k : 12 * k + 12] for k in range(len(CHUNKS))]
-    state, codes, held, link_send, link_recv, own_sem, peer_sem, peer_send, misc = scratch[12 * len(CHUNKS) :]
+    state, early, late, codes, held, link_send, link_recv, own_sem, peer_sem, peer_send, misc = scratch[12 * len(CHUNKS) :]
     group, fsdp = lax.axis_index("group"), lax.axis_index("fsdp")
     core = group % 2
     here = (fsdp // 4 % 4, fsdp // 16 * 2 + group // 2, fsdp % 4)
@@ -108,6 +109,8 @@
         first, sizes = CHUNKS[k]
         out, at_row = [], 0
         for order, rows in zip(ORDERS, sizes):
+            if rows == 0:
+                continue
             cut = 8 * ((rows // 8 + odd) // 2)
             out.append((order, at_row, at_row + cut, at_row + rows, first + at_row))
             at_row += rows
@@ -128,27 +131,29 @@
     def arrived(ref, sem):
         pltpu.make_async_copy(ref, ref, sem).wait()
 
-    def terms(k, slots, which):
+    def terms(k, slots, which, odd=0, way=None):
         each = sum(CHUNKS[k][1]) // 2
-        for order, low, _, high, first in parts_of(k):
+        for order, low, cut, high, first in parts_of(k, odd):
+            if way is not None:
+                low, high = ((low, cut), (cut, high))[way]
             slot = {axis: slots[i] for i, axis in enumerate(order)}
             start = starts[0][slot[0]] + starts[1][slot[1]] + starts[2][slot[2]] + which * HALF + CHUNKS[k][0]
             for g in range(2):
                 begin, end = max(low, g * each), min(high, (g + 1) * each)
                 if begin < end:
                     rows = pl.ds(pl.multiple_of(start + (begin - g * each), 8), end - begin)
-                    yield grads.at[rows, group_rows[slot[1]] + g], slots + (pl.ds(begin, end - begin),)
+                    yield grads.at[rows, group_rows[slot[1]] + g], slots + (pl.ds(begin, end - begin),), order[0]
 
     def load(k, g):
         for m in range(4):
             for s in slots_of(LOADS[k][g]):
-                for source, place in terms(k, (m,) + s, core):
+                for source, place, _ in terms(k, (m,) + s, core):
                     pltpu.make_async_copy(source, bufs[k][0].at[place], own_sem.at[sum(LOADED[:k]) + g]).start()
 
     def give_peer(k, block, slots, sem):
         for m in slots:
             for s in slots_of(block):
-                for source, place in terms(k, (m,) + s, 1 - core):
+                for source, place, _ in terms(k, (m,) + s, 1 - core):
                     pltpu.make_async_remote_copy(
                         src_ref=source,
                         dst_ref=bufs[k][1].at[place],
@@ -222,7 +227,37 @@
         for order, low, cut, high, _ in parts_of(k, u % 2):
             axis = order[stage]
             for rows, to in (((low, cut), ahead[axis]), ((cut, high), behind[axis])):
+                if rows[0] == rows[1]:
+                    continue
                 send(k, stage, u, 0, values(k, stage, u, FAR, rows), far(k, stage, u, rows), to)
+
+    def send_raw(k, u):
+        for which, target, kinds in (
+            (core, bufs[k][2], (link_send.at[3 * k], landing(k, 0, u, 0))),
+            (1 - core, early, (misc.at[5 + 3 * len(CHUNKS)], misc.at[6 + 3 * len(CHUNKS)])),
+        ):
+            for s in slots_of(UNITS[k][u]):
+                for way, to in enumerate((ahead, behind)):
+                    for source, place, axis in terms(k, (FAR,) + s, which, u % 2, way):
+                        pltpu.make_async_remote_copy(
+                            src_ref=source,
+                            dst_ref=target.at[place[1:]],
+                            send_sem=kinds[0],
+                            recv_sem=kinds[1],
+                            device_id=to[axis],
+                            device_id_type=MESH,
+                        ).start()
+
+    def hand_over(k, u):
+        arrived(at(early, (), UNITS[k][u]), misc.at[6 + 3 * len(CHUNKS)])
+        pltpu.make_async_remote_copy(
+            src_ref=at(early, (), UNITS[k][u]),
+            dst_ref=at(late, (), UNITS[k][u]),
+            send_sem=peer_send.at[k],
+            recv_sem=misc.at[7 + 3 * len(CHUNKS)],
+            device_id=other_core,
+            device_id_type=MESH,
+        ).start()
 
     def send_near(k, stage, u):
         if stage == 0:
@@ -230,15 +265,23 @@
         for order, low, cut, high, _ in parts_of(k, u % 2):
             axis = order[stage]
             for slot, way, rows, to in ((AFTER, 0, (cut, high), ahead[axis]), (BEFORE, 1, (low, cut), behind[axis])):
+                if rows[0] == rows[1]:
+                    continue
                 sum_up(k, stage, u, slot, rows, [])
                 send(k, stage, u, 1, values(k, stage, u, slot, rows), near(k, stage, u, way, rows), to)
 
     def pass_on(k, stage, u):
         arrived(far(k, stage, u), landing(k, stage, u, 0))
+        came = [(bufs[k][2 + 2 * stage], ())]
+        if stage == 0 and (k, u) == RAW:
+            arrived(at(late, (), UNITS[k][u]), misc.at[7 + 3 * len(CHUNKS)])
+            came.append((late, ()))
         for order, low, cut, high, _ in parts_of(k, u % 2):
             axis = order[stage]
             for slot, way, rows, to in ((AFTER, 0, (low, cut), ahead[axis]), (BEFORE, 1, (cut, high), behind[axis])):
-                sum_up(k, stage, u, slot, rows, [(bufs[k][2 + 2 * stage], ())])
+                if rows[0] == rows[1]:
+                    continue
+                sum_up(k, stage, u, slot, rows, came)
                 send(k, stage, u, 1, values(k, stage, u, slot, rows), near(k, stage, u, way, rows), to)
 
     def finish(k, stage, u):
@@ -301,9 +344,13 @@
             new.at[g, 2][...] = second_moment
         total = lambda w: w[0] * new_params[0] + w[1] * new_params[1]
         by_device = known["weights"]
-        for c in range(2):
+        for c in (1, 0):
             sums.at[2 + c][...] = total(by_device[2 + c])
-            push(k, sums.at[2 + c], landed.at[core], 1, across[c])
+        push(k, sums.at[3], landed.at[core], 1, across[1])
+        known["order"] = known.get("order", []) + [k]
+        if len(known["order"]) == len(CHUNKS):
+            for j in known["order"]:
+                push(j, bufs[j][9].at[2], bufs[j][11].at[core], 1, across[0])
         sums.at[1][...] = total(by_device[1])
         push(k, sums.at[1], beside.at[3], 0, other_core)
         push(k, new.at[1 - core], beside.at[pl.ds(0, 3)], 0, other_core)
@@ -330,7 +377,8 @@
         "g": lambda k, u: give_peer(k, UNITS[k][u], (FAR,), given(k, 0, u)),
         "h": lambda k, u: give_peer(k, UNITS[k][u], (AFTER, BEFORE), given(k, 1, u)),
         "G": lambda k, g: give_peer(k, LOADS[k][g], (OWN,), given(k, 2, g)),
-        "b": lambda k, u: send_far(k, 0, u),
+        "b": lambda k, u: send_raw(k, u) if (k, u) == RAW else send_far(k, 0, u),
+        "x": hand_over,
         "c": lambda k, u: send_near(k, 0, u),
         "d": lambda k, u: pass_on(k, 0, u),
         "o": lambda k, u: finish(k, 0, u),
@@ -357,9 +405,9 @@
     pltpu.make_async_copy(holders, held, misc.at[3]).start()
     pl.semaphore_wait(barrier, 8)
     plan = " ".join(PLAN).split()
-    early = 12
+    state_at = 12
     for number, step in enumerate(plan):
-        if number == early:
+        if number == state_at:
             for i, ref in enumerate((params, one, two)):
                 pltpu.make_async_remote_copy(
                     src_ref=ref.at[other_half],
@@ -371,6 +419,7 @@
                 ).start()
         if step[1] == "t" and step == [s for s in plan if s[1] == "t"][-1]:
             arrived(state.at[0], misc.at[4 + 3 * len(CHUNKS)])
+            arrived(at(early, (), UNITS[RAW[0]][RAW[1]]), misc.at[5 + 3 * len(CHUNKS)])
             for k in range(len(CHUNKS)):
                 arrived(bufs[k][0], peer_send.at[k])
                 arrived(bufs[k][0].at[pl.ds(0, 3)], link_send.at[3 * k])
@@ -407,6 +456,8 @@
     chunks = len(CHUNKS)
     scratch += [
         pltpu.VMEM((2, 3, HALF, LANES), f32),
+        pltpu.VMEM((4, 4, sum(CHUNKS[RAW[0]][1]), LANES), f32),
+        pltpu.VMEM((4, 4, sum(CHUNKS[RAW[0]][1]), LANES), f32),
         pltpu.SMEM((2, 4), f32),
         pltpu.SMEM((1, 2), jnp.int32),
         pltpu.SemaphoreType.DMA((chunks * 3,)),
@@ -414,7 +465,7 @@
         pltpu.SemaphoreType.DMA((sum(LOADED),)),
         pltpu.SemaphoreType.DMA((sum(GIVEN),)),
         pltpu.SemaphoreType.DMA((chunks,)),
-        pltpu.SemaphoreType.DMA((5 + 3 * chunks,)),
+        pltpu.SemaphoreType.DMA((8 + 3 * chunks,)),
     ]
     results = pl.pallas_call(
         kernel,

time: 48 us -> 47.1 us (0.981)
  Pallas kernels: 47.2 us -> 46 us
    pallas_call x1, Pallas kernels: 46.4 us -> 45.1 us  [shards(): pl.pallas_call(kernel, out_shape=pltpu.VMEM((4, ROWS, LANES), f32), in_sp...]
where the time goes in v5:
time: 47.1 us; the launch traced here: 46.6 us
  Pallas kernels  46 us (98%)
  between operations  0.64 us (1%)
    pallas_call x1, Pallas kernels, shards(): pl.pallas_call(kernel, out_shape=pltpu.VMEM((4, ROWS, LANES), f32), in_sp...  45.1 us

profile of v5, /device:TPU:1, one launch (start us, length us, event | category | flops | bytes accessed | tf_op | source)
XLA Modules:
  0.0 46.6 jit_solution(6883468483144047858)
XLA Ops:
  0.6 45.1 %shard_map.93.results = f32[4,256,128]{2,1,0:T(8,128)S(1)} custom-call(f32[8192,4,128]{2,1,0:T(4,128)} %bitcast.11, f32[256,128]{1,0:T(8,128)} %bitcast.12, f32[256,128]{1,0:T(8,128)} %bitcast.13, f32[256,128]{1,0:T(8,128)} %bitcast.14, f32[2,4]{1,0:T(2,128)} %bitcast.15, s32[1,2]{1,0:T(1,128)} %holders.1), custom_call_target="tpu_custom_call" | custom-call | tf_op jit(solution)/shard_map/pallas_call | solution.py:470
  45.8 0.8 %shard_map.94 = (f32[256,128]{1,0:T(8,128)}, f32[256,128]{1,0:T(8,128)}, f32[256,128]{1,0:T(8,128)}, f32[256,128]{1,0:T(8,128)}) custom-call(f32[4,256,128]{2,1,0:T(8,128)S(1)} %shard_map.93.results), custom_call_target="tpu_custom_call" | custom-call | tf_op jit(solution)/shard_map/pallas_call | solution.py:480

commit v6 on v5

--- a/solution.py
+++ b/solution.py
@@ -331,7 +331,7 @@
         mine = pl.ds(CHUNKS[k][0], each)
         first_fix = 1.0 - 0.9**10
         second_fix = 1.0 - 0.95**10
-        new_params = []
+        new_params, moments = [], []
         for g in range(2):
             gradient = bufs[k][0].at[OWN, OWN, OWN, pl.ds(g * each, each)][...]
             values = state.at[g, 0, mine][...]
@@ -339,18 +339,19 @@
             second_moment = 0.95 * state.at[g, 2, mine][...] + 0.05 * gradient * gradient
             update = first_moment / first_fix / (jnp.sqrt(second_moment / second_fix) + 1e-08) + 0.1 * values
             new_params.append(values - 0.05 * update)
-            new.at[g, 0][...] = new_params[g]
-            new.at[g, 1][...] = first_moment
-            new.at[g, 2][...] = second_moment
+            moments.append((first_moment, second_moment))
         total = lambda w: w[0] * new_params[0] + w[1] * new_params[1]
         by_device = known["weights"]
-        for c in (1, 0):
-            sums.at[2 + c][...] = total(by_device[2 + c])
+        sums.at[3][...] = total(by_device[3])
         push(k, sums.at[3], landed.at[core], 1, across[1])
+        sums.at[2][...] = total(by_device[2])
         known["order"] = known.get("order", []) + [k]
         if len(known["order"]) == len(CHUNKS):
             for j in known["order"]:
                 push(j, bufs[j][9].at[2], bufs[j][11].at[core], 1, across[0])
+        for g in range(2):
+            new.at[g, 0][...] = new_params[g]
+            new.at[g, 1][...], new.at[g, 2][...] = moments[g]
         sums.at[1][...] = total(by_device[1])
         push(k, sums.at[1], beside.at[3], 0, other_core)
         push(k, new.at[1 - core], beside.at[pl.ds(0, 3)], 0, other_core)

time: 47.1 us -> 47.1 us (level)
  no operation moved by 1% of the time
where the time goes in v6:
time: 47.1 us; the launch traced here: 46.6 us
  Pallas kernels  46 us (98%)
  between operations  0.64 us (1%)
    pallas_call x1, Pallas kernels, shards(): pl.pallas_call(kernel, out_shape=pltpu.VMEM((4, ROWS, LANES), f32), in_sp...  45.1 us

profile of v6, /device:TPU:1, one launch (start us, length us, event | category | flops | bytes accessed | tf_op | source)
XLA Modules:
  0.0 46.6 jit_solution(16335776545349892838)
XLA Ops:
  0.6 45.1 %shard_map.93.results = f32[4,256,128]{2,1,0:T(8,128)S(1)} custom-call(f32[8192,4,128]{2,1,0:T(4,128)} %bitcast.11, f32[256,128]{1,0:T(8,128)} %bitcast.12, f32[256,128]{1,0:T(8,128)} %bitcast.13, f32[256,128]{1,0:T(8,128)} %bitcast.14, f32[2,4]{1,0:T(2,128)} %bitcast.15, s32[1,2]{1,0:T(1,128)} %holders.1), custom_call_target="tpu_custom_call" | custom-call | tf_op jit(solution)/shard_map/pallas_call | solution.py:471
  45.8 0.8 %shard_map.94 = (f32[256,128]{1,0:T(8,128)}, f32[256,128]{1,0:T(8,128)}, f32[256,128]{1,0:T(8,128)}, f32[256,128]{1,0:T(8,128)}) custom-call(f32[4,256,128]{2,1,0:T(8,128)S(1)} %shard_map.93.results), custom_call_target="tpu_custom_call" | custom-call | tf_op jit(solution)/shard_map/pallas_call | solution.py:481
